TPU v7x, 512 devices: a whole 4x8x8 slice. The times are simulated.
512 devices in a mesh: dp: 4 (over x), ctx: 4 (over y_lo), vocab: 32 (over y_hi, z, core).
Axes of the slice: x: 4, y: 8 (y_hi: 2, y_lo: 4; y = y_hi * 4 + y_lo), z: 8, core: 2. Of those that a mesh axis runs over, the one named last changes fastest.
Arguments:
- hidden: bfloat16 [4, 256, 2048], P('dp', 'ctx'), may hold values from -32 to 32
- head_weight: bfloat16 [114688, 2048], P(('ctx', 'vocab')), may hold values from -12 to 12
- labels: int32 [4, 256], P('dp'), may hold values from 0 to 114687
- loss_mask: int32 [4, 256], P('dp'), may hold values from 0 to 1
- seq_ids: int32 [4, 256], P('dp'), may hold values from 0 to 7, as said below
- old_logp: float32 [4, 256], P('dp'), may hold values from -20 to 0
- ref_logp: float32 [4, 256], P('dp'), may hold values from -20 to -13.5
- advantages: float32 [4, 8], P('dp'), may hold values from -4 to 4
Outputs:
- hidden_grad: bfloat16 [4, 256, 2048], P('dp', 'ctx', 'vocab')
- head_grad: bfloat16 [114688, 2048], P(('ctx', 'vocab'), 'dp')
Inputs may be any that keep to these rules, and one draw needn't show every extreme that they name: seq_ids never fall along a window, and every sequence number from 0 to 7 occurs in each window.
All inputs are finite; a program needn't handle non-finite values.
Results may differ from a plain program's by a relative error of at most 0.035.
Values may be sent and summed in bfloat16 or wider, within the bound.
A program may use at most 64 MiB of HBM per device.

v0:
```python
import jax
import jax.numpy as jnp
from jax import lax
from jax.sharding import PartitionSpec as P

CLIP_LOW = 0.2
CLIP_HIGH = 0.28
DUAL_CLIP = 3.0
KL_COEF = 0.04
KL_CAP = 10.0
LOSS_SCALE = 64.0


def token_weights(logp, targets_mask, seq_row, old_row, ref_row, adv_row):
    seq_match = (seq_row[:, None] == jnp.arange(adv_row.shape[0], dtype=jnp.int32)[None, :]).astype(
        jnp.float32
    )
    lengths = jnp.sum(seq_match, axis=0)
    token_adv = jnp.sum(seq_match * adv_row[None, :], axis=1)
    token_len = jnp.sum(seq_match * lengths[None, :], axis=1)
    prob_ratio = jnp.exp(logp - old_row)
    active = jnp.where(
        token_adv >= 0.0,
        prob_ratio <= 1.0 + CLIP_HIGH,
        (prob_ratio >= 1.0 - CLIP_LOW) & (prob_ratio <= DUAL_CLIP),
    )
    policy_term = jnp.where(active, -token_adv * prob_ratio, 0.0)
    log_gap = ref_row - logp
    exp_gap = jnp.exp(log_gap)
    kl_value = exp_gap - log_gap - 1.0
    penalty = jnp.where(kl_value < KL_CAP, 1.0 - exp_gap, 0.0)
    return (
        LOSS_SCALE
        * targets_mask.astype(jnp.float32)
        * (policy_term + KL_COEF * penalty)
        / token_len
    )


def body(hidden, head_weight, labels, loss_mask, seq_ids, old_logp, ref_logp, advantages):
    window = lax.all_gather(hidden, "ctx", axis=1, tiled=True)[0]
    window_len = window.shape[0]
    width = window.shape[1]
    shard_rows = head_weight.shape[0]
    logits = jnp.dot(window, head_weight.T, preferred_element_type=jnp.float32)
    base_index = (
        lax.axis_index("ctx") * lax.axis_size("vocab") + lax.axis_index("vocab")
    ) * shard_rows
    columns = base_index + lax.iota(jnp.int32, shard_rows)
    label_hit = labels[0][:, None] == columns[None, :]
    local_label = jnp.sum(jnp.where(label_hit, logits, 0.0), axis=1)
    local_max = jnp.max(logits, axis=1)
    global_max = lax.pmax(local_max, ("ctx", "vocab"))
    local_sum = jnp.sum(jnp.exp(logits - global_max[:, None]), axis=1)
    sum_total, label_logit = lax.psum((local_sum, local_label), ("ctx", "vocab"))
    log_total = global_max + jnp.log(sum_total)
    token_grad = token_weights(
        label_logit - log_total, loss_mask[0], seq_ids[0], old_logp[0], ref_logp[0], advantages[0]
    )
    likely = jnp.exp(logits - log_total[:, None])
    grad_logits = (token_grad[:, None] * (label_hit.astype(jnp.float32) - likely)).astype(
        jnp.bfloat16
    )
    groups = lax.axis_size("dp")
    slice_width = width // groups
    pieces = window.reshape(window_len, groups, slice_width)
    repeated = jnp.broadcast_to(grad_logits[:, None, :], (window_len, groups, shard_rows))
    payload = jnp.concatenate([repeated, pieces], axis=2)
    received = lax.all_to_all(payload, "dp", split_axis=1, concat_axis=1, tiled=True)
    shared_grads = received[:, :, :shard_rows]
    shared_cols = received[:, :, shard_rows:]
    head_grad = lax.dot_general(
        shared_grads, shared_cols, (((0, 1), (0, 1)), ((), ())), preferred_element_type=jnp.float32
    ).astype(jnp.bfloat16)
    partial_value = jnp.dot(grad_logits, head_weight, preferred_element_type=jnp.float32)
    ctx_count = lax.axis_size("ctx")
    vocab_count = lax.axis_size("vocab")
    block_len = window_len // ctx_count
    part_width = width // vocab_count
    contrib = partial_value.reshape(ctx_count, block_len, vocab_count, part_width)
    contrib = contrib.transpose(0, 2, 1, 3).reshape(ctx_count * vocab_count * block_len, part_width)
    state_grad = lax.psum_scatter(contrib, ("ctx", "vocab"), scatter_dimension=0, tiled=True)
    return (state_grad.astype(jnp.bfloat16)[None], head_grad)


def solution(mesh):
    placed = (
        P("dp", "ctx", None),
        P(("ctx", "vocab"), None),
        P("dp", None),
        P("dp", None),
        P("dp", None),
        P("dp", None),
        P("dp", None),
        P("dp", None),
    )
    return jax.shard_map(
        body,
        mesh=mesh,
        in_specs=placed,
        out_specs=(P("dp", "ctx", "vocab"), P(("ctx", "vocab"), "dp")),
        check_vma=False,
    )
```

profile of v0, /device:TPU:54, one launch (start us, length us, event | category | flops | bytes accessed | tf_op | source)
XLA Modules:
  0.0 1426.9 jit_solution(18224944553554929168)
XLA Ops:
  7.2 0.0 all-gather.2.cloned.1.call-start
  7.2 0.7 all-gather.2.cloned.1.call-update
  7.9 0.0 reduce-scatter.2.cloned.1.call-start
  8.0 0.8 convert_reduce_fusion
  8.8 0.8 select_reduce_fusion.1
  9.5 0.7 convert_multiply_fusion
  10.2 37.8 %all-gather.2.cloned.1.call-done = bf16[1,256,2048]{2,1,0:T(8,128)(2,1)} async-done(((bf16[1,64,2048]{2,1,0:T(8,128)(2,1)}), bf16[1,256,2048]{2,1,0:T(8,128)(2,1)}) %all-gather.2.cloned.1.call-update) | async-done | bytes 1048592 | tf_op jit(solution)/shard_map/all_gather | solution.py:41
  48.0 3.7 fusion.16
  51.7 339.1 %pmax.7 = f32[256]{0:T(256)S(1)} all-reduce(f32[256]{0:T(256)S(1)} %get-tuple-element.10), channel_id=1, replica_groups=mesh['dp'=4,'ctx'=4,'vocab'=32] {'ctx','vocab'}, use_global_device_ids=true, to_apply=%region_4.5 | all-reduce | flops 256 | bytes 2048 | tf_op jit(solution)/shard_map/pmax | solution.py:53
  390.8 0.4 fusion.7
  391.2 333.1 %all-reduce = (f32[256]{0:T(256)S(1)}, f32[256]{0:T(256)S(1)}) all-reduce(f32[256]{0:T(256)S(1)} %get-tuple-element.3, f32[256]{0:T(256)S(1)} %get-tuple-element.2), channel_id=1, replica_groups=mesh['dp'=4,'ctx'=4,'vocab'=32] {'ctx','vocab'}, use_global_device_ids=true, to_apply=%region_6.7 | all-reduce | flops 512 | bytes 4096 | tf_op jit(solution)/shard_map/psum | solution.py:55
  724.4 0.3 fusion.10
  724.7 3.3 fusion.17
  728.0 3.0 reshape.24
  731.1 6.5 copy.20
  737.7 1.2 copy-done
  738.9 0.5 copy.21
  739.4 0.5 copy.22
  739.9 0.1 broadcast_in_dim.13
  740.1 0.2 pad_maximum_fusion
  740.3 37.3 %all_to_all.5 = bf16[256,4,1408]{2,0,1:T(8,128)(2,1)S(1)} all-to-all(bf16[256,4,1408]{2,0,1:T(8,128)(2,1)S(1)} %pad_maximum_fusion), channel_id=1, replica_groups=mesh['dp'=4,'ctx'=4,'vocab'=32] {'dp'}, dimensions={1} | all-to-all | bytes 5767168 | tf_op jit(solution)/shard_map/all_to_all | solution.py:69
  777.6 2.1 bitcast_convert_fusion
  779.7 639.0 %reduce-scatter.2.cloned.1.call-done = f32[64,64]{1,0:T(8,128)} async-done(((f32[8192,64]{1,0:T(8,128)}), f32[64,64]{1,0:T(8,128)}) %reduce-scatter.2.cloned.1.call-update) | async-done | bytes 16400 | tf_op jit(solution)/shard_map/reduce_scatter | solution.py:82
  1418.7 1.4 convert_bitcast_fusion
  (10 shorter events, 0.1 us)
Async XLA Ops:
  7.2 40.9 %all-gather.2.cloned.1.call-start = ((), (), s32[]{:S(2)}) async-start(), calls=%async_computation.2 | async-start | bytes 1310720 | tf_op jit(solution)/shard_map/all_gather | solution.py:41
  7.9 1410.8 %reduce-scatter.2.cloned.1.call-start = ((), (), s32[]{:S(2)}) async-start(), calls=%async_computation.3 | async-start | bytes 4227072 | tf_op jit(solution)/shard_map/reduce_scatter | solution.py:82
  10.2 380.6 %copy-start.1 = (s32[1,256]{1,0:T(1,128)S(1)}, s32[1,256]{1,0:T(1,128)}, u32[]{:S(2)}) copy-start(s32[1,256]{1,0:T(1,128)} %param.10) | copy-start | bytes 3076
  10.2 714.1 %copy-start.2 = (f32[1,256]{1,0:T(1,128)S(1)}, f32[1,256]{1,0:T(1,128)}, u32[]{:S(2)}) copy-start(f32[1,256]{1,0:T(1,128)} %param.14) | copy-start | bytes 3076
  10.2 714.1 %copy-start.3 = (f32[1,256]{1,0:T(1,128)S(1)}, f32[1,256]{1,0:T(1,128)}, u32[]{:S(2)}) copy-start(f32[1,256]{1,0:T(1,128)} %param.13) | copy-start | bytes 3076
  737.6 1.2 copy-start
Sparse Core Ops, SparseCore 0:
  10.1 37.8 all-gather.1
  737.8 680.8 reduce-scatter.1
where the time goes:
time: 1430 us
  blocking collectives  710 us (50%)
  waiting for transfers between devices  678 us (47%)
    reduce_scatter x1, waiting for transfers between devices, body(): lax.psum_scatter(contrib, ('ctx', 'vocab'), scatter_dimension=0, tiled=True)  639 us
    pmax x1, blocking collectives, body(): global_max = lax.pmax(local_max, ('ctx', 'vocab'))  339 us
    psum x1, blocking collectives, body(): lax.psum((local_sum, local_label), ('ctx', 'vocab'))  333 us
    all_gather x1, waiting for transfers between devices, body(): window = lax.all_gather(hidden, 'ctx', axis=1, tiled=True)[0]  37.8 us
    all_to_all x1, blocking collectives, body(): lax.all_to_all(payload, 'dp', split_axis=1, concat_axis=1, tiled=True)  37.3 us
  transfers between devices with their start and end apart: 2, of which 2 were waited for; matrix products, arithmetic and copies ran while one was open for 0% of the time, Pallas kernels for 0%

commit v1 on v0

v1 whole, which is shorter than its diff:
```python
import functools

import jax
import jax.numpy as jnp
from jax import lax
from jax.experimental import pallas as pl
from jax.experimental.pallas import tpu as pltpu
from jax.sharding import PartitionSpec as P

CLIP_LOW = 0.2
CLIP_HIGH = 0.28
DUAL_CLIP = 3.0
KL_COEF = 0.04
KL_CAP = 10.0
LOSS_SCALE = 64.0

MESH = pl.DeviceIdType.MESH
F32 = jnp.float32
BF16 = jnp.bfloat16

NX = 4
NC = 4
NH = 2
NY = NC * NH
NZ = 8
WIN = 256
TOK = WIN // NC
HALF = TOK // 2
QTR = HALF // 2
D = 2048
ROWS = 896
CH = 128
COLS = D // NX
PART = 512
NPART = D // PART
SPLIT = ROWS // 2


def token_weights(logp, mask, seq, old, ref, adv_ref):
    adv = jnp.zeros_like(logp)
    length = jnp.zeros_like(logp)
    for s in range(adv_ref.shape[1]):
        match = (seq == s).astype(F32)
        count = jnp.sum(match, axis=1, keepdims=True)
        adv = adv + match * adv_ref[0:1, s : s + 1]
        length = length + match * count
    ratio = jnp.exp(logp - old)
    low = jnp.where(ratio >= 1.0 - CLIP_LOW, jnp.where(ratio <= DUAL_CLIP, 1.0, 0.0), 0.0)
    active = jnp.where(adv >= 0.0, jnp.where(ratio <= 1.0 + CLIP_HIGH, 1.0, 0.0), low)
    policy = jnp.where(active > 0.0, -adv * ratio, 0.0)
    gap = ref - logp
    exp_gap = jnp.exp(gap)
    penalty = jnp.where(exp_gap - gap - 1.0 < KL_CAP, 1.0 - exp_gap, 0.0)
    return LOSS_SCALE * mask.astype(F32) * (policy + KL_COEF * penalty) / length


def merge(ref, n):
    top = ref[0, 0:2, :]
    for i in range(1, n):
        top = jnp.maximum(top, ref[i, 0:2, :])
    total = jnp.zeros_like(top)
    label = jnp.zeros_like(top)
    for i in range(n):
        total = total + ref[i, 2:4, :] * jnp.exp(ref[i, 0:2, :] - top)
        label = label + ref[i, 4:6, :]
    return top, total, label


def put(ref, slot, top, total, label):
    ref[slot] = jnp.concatenate([top, total, label, jnp.zeros_like(top)], axis=0)


def fold(row):
    return jnp.concatenate([row[:, :128], row[:, 128:]], axis=0)


def unfold(tile):
    return jnp.concatenate([tile[0:1, :], tile[1:2, :]], axis=1)


def kernel(
    hid_ref,
    w_hbm,
    lab_ref,
    mask_ref,
    seq_ref,
    old_ref,
    refp_ref,
    adv_ref,
    hg_ref,
    head_hbm,
    w,
    win,
    hc,
    logit,
    q,
    gt,
    g,
    keep,
    e1s,
    e1r,
    rsa,
    rsb,
    ra1,
    rb1,
    ra2s,
    rb2s,
    ra2,
    rb2,
    fin,
    st0,
    st1,
    st2,
    scale,
    acc,
    head,
    loc_sem,
    a_send,
    a_recv,
    f_send,
    f_recv,
    h_send,
    h_recv,
    hf_send,
    hf_recv,
    q_send,
    q_recv,
    c0_send,
    c0_recv,
    c1_send,
    c1_recv,
    c2_send,
    c2_recv,
    x_send,
    x_recv,
    e_send,
    e_recv,
    ra1_send,
    ra1_recv,
    rb1_send,
    rb1_recv,
    ra2_send,
    ra2_recv,
    rb2_send,
    rb2_recv,
    fin_send,
    fin_recv,
):
    x = lax.axis_index("dp")
    c = lax.axis_index("ctx")
    v = lax.axis_index("vocab")
    h = v // (NZ * 2)
    z = (v // 2) % NZ
    k = v % 2
    y = h * NC + c

    def at_y(to):
        return (x, to % NC, (to // NC) * (NZ * 2) + z * 2 + k)

    def at_z(to):
        return (x, c, h * (NZ * 2) + to * 2 + k)

    def at_x(to):
        return (to, c, v)

    partner = (x, c, h * (NZ * 2) + z * 2 + (1 - k))

    def send(src, dst, ssem, rsem, to):
        copy = pltpu.make_async_remote_copy(
            src_ref=src, dst_ref=dst, send_sem=ssem, recv_sem=rsem, device_id=to, device_id_type=MESH
        )
        copy.start()
        return copy

    def arrived(dst, ssem, rsem, to):
        pltpu.make_async_remote_copy(
            src_ref=dst, dst_ref=dst, send_sem=ssem, recv_sem=rsem, device_id=to, device_id_type=MESH
        ).wait_recv()

    sent = []

    load_w = pltpu.make_async_copy(w_hbm, w, loc_sem.at[0])
    load_w.start()

    barrier = pltpu.get_barrier_semaphore()
    peers = [partner]
    peers += [at_y((y + d) % NY) for d in range(1, NY)]
    peers += [at_z((z + d) % NZ) for d in range(1, NZ)]
    peers += [at_x((x + d) % NX) for d in range(1, NX)]
    for peer in peers:
        pl.semaphore_signal(barrier, inc=1, device_id=peer, device_id_type=MESH)
    win[pl.ds(pl.multiple_of(c * TOK, TOK), TOK), :] = hid_ref[0]
    pl.semaphore_wait(barrier, len(peers))

    def half_block(block, half):
        return win.at[pl.ds(pl.multiple_of(block * TOK + half * HALF, HALF), HALF), :]

    mine = half_block(c, k)
    far = (y + NY + 2 - 4 * k) % NY
    for i, to in enumerate(((y + 1) % NY, (y + NY - 1) % NY, far)):
        sent.append(send(mine, mine, a_send.at[i], a_recv.at[i], at_y(to)))
    from_block = ((c + NC - 1) % NC, (c + 1) % NC, (c + 2) % NC)
    for i in range(3):
        piece = half_block(from_block[i], k)
        arrived(piece, a_send.at[i], a_recv.at[i], partner)
        sent.append(send(piece, piece, f_send.at[i], f_recv.at[i], partner))
    for i in range(3):
        piece = half_block(from_block[i], 1 - k)
        arrived(piece, f_send.at[i], f_recv.at[i], partner)

    half_win = pl.ds(pl.multiple_of(k * (WIN // 2), WIN // 2), WIN // 2)
    other_win = pl.ds(pl.multiple_of((1 - k) * (WIN // 2), WIN // 2), WIN // 2)
    place = {0: 0, 1: 1, 3: 2, 2: 3}
    for d in (1, 3, 2):
        to = (x + d) % NX
        src = win.at[half_win, pl.ds(pl.multiple_of(to * COLS, COLS), COLS)]
        dst = hc.at[place[d], half_win, :]
        sent.append(send(src, dst, h_send.at[d - 1], h_recv.at[d - 1], at_x(to)))

    load_w.wait()
    logit[...] = lax.dot_general(
        w[...], win[...], (((1,), (1,)), ((), ())), preferred_element_type=F32
    )
    base = (c * (NH * NZ * 2) + v) * ROWS
    local_label = lab_ref[...] - base

    def hit(i):
        rows = lax.broadcasted_iota(jnp.int32, (CH, WIN), 0) + i * CH
        return rows == local_label

    def rows_of(i):
        return pl.ds(pl.multiple_of(i * CH, CH), CH)

    def stat_step(i, carry):
        top, label = carry
        part = logit[rows_of(i), :]
        top = jnp.maximum(top, jnp.max(part, axis=0, keepdims=True))
        label = label + jnp.sum(jnp.where(hit(i), part, 0.0), axis=0, keepdims=True)
        return top, label

    top, label = lax.fori_loop(
        0, ROWS // CH, stat_step, (jnp.full((1, WIN), -jnp.inf, F32), jnp.zeros((1, WIN), F32))
    )

    def exp_step(i, total):
        part = jnp.exp(logit[rows_of(i), :] - top)
        q[0, rows_of(i), :] = jnp.where(hit(i), -1.0, part).astype(BF16)
        return total + jnp.sum(part, axis=0, keepdims=True)

    total = lax.fori_loop(0, ROWS // CH, exp_step, jnp.zeros((1, WIN), F32))

    put(st0, k, fold(top), fold(total), fold(label))
    sent.append(send(st0.at[k], st0.at[k], c0_send, c0_recv, partner))

    right, left = (x + 1) % NX, (x + NX - 1) % NX
    lo, hi = pl.ds(0, SPLIT), pl.ds(SPLIT, SPLIT)
    sent.append(send(q.at[0, lo, :], q.at[1, lo, :], q_send.at[0], q_recv.at[0], at_x(right)))
    sent.append(send(q.at[0, hi, :], q.at[2, hi, :], q_send.at[1], q_recv.at[1], at_x(left)))
    sent.append(send(q.at[0, hi, :], q.at[1, hi, :], q_send.at[2], q_recv.at[2], at_x(right)))
    sent.append(send(q.at[0, lo, :], q.at[2, lo, :], q_send.at[3], q_recv.at[3], at_x(left)))

    arrived(st0.at[1 - k], c0_send, c0_recv, partner)
    put(st1, y, *merge(st0, 2))
    for d in range(1, NY):
        to = (y + d) % NY
        sent.append(send(st1.at[y], st1.at[y], c1_send.at[d - 1], c1_recv.at[d - 1], at_y(to)))
    for d in range(1, NY):
        arrived(st1.at[(y + NY - d) % NY], c1_send.at[d - 1], c1_recv.at[d - 1], partner)
    put(st2, z, *merge(st1, NY))
    for d in range(1, NZ):
        to = (z + d) % NZ
        sent.append(send(st2.at[z], st2.at[z], c2_send.at[d - 1], c2_recv.at[d - 1], at_z(to)))
    for d in range(1, NZ):
        arrived(st2.at[(z + NZ - d) % NZ], c2_send.at[d - 1], c2_recv.at[d - 1], partner)
    all_top, all_total, all_label = merge(st2, NZ)
    log_total = unfold(all_top + jnp.log(all_total))
    logp = unfold(all_label) - log_total
    coeff = token_weights(
        logp, mask_ref[...], seq_ref[...], old_ref[...], refp_ref[...], adv_ref
    )

    factor = coeff * jnp.exp(top - log_total)
    label_grad = coeff * (1.0 - jnp.exp(logp))
    put(scale, 0, fold(factor), fold(label_grad), fold(label_grad))
    for d in (1, 3, 2):
        sent.append(
            send(scale.at[0], scale.at[d], x_send.at[d - 1], x_recv.at[d - 1], at_x((x + d) % NX))
        )

    def grad_step(i, carry):
        grad = coeff * (hit(i).astype(F32) - jnp.exp(logit[rows_of(i), :] - log_total))
        gt[rows_of(i), 0:WIN] = grad.astype(BF16)
        turned = grad.T.astype(BF16)
        for j in range(NC):
            for half in range(2):
                row = j * HALF + (WIN // 2) * (k if half else 1 - k)
                start = j * TOK + half * HALF
                g[pl.ds(pl.multiple_of(row, HALF), HALF), rows_of(i)] = turned[start : start + HALF]
        return carry

    lax.fori_loop(0, ROWS // CH, grad_step, 0)

    for n in range(NPART):
        cols = pl.ds(n * PART, PART)
        value = jnp.dot(g[...], w[:, n * PART : (n + 1) * PART], preferred_element_type=F32)
        e1s[:, cols] = value[: WIN // 2].astype(BF16)
        keep[:, cols] = value[WIN // 2 :]
        sent.append(send(e1s.at[:, cols], e1r.at[:, cols], e_send.at[n], e_recv.at[n], partner))

    arrived(q.at[1, lo, :], q_send.at[0], q_recv.at[0], partner)
    sent.append(send(q.at[1, lo, :], q.at[3, lo, :], q_send.at[4], q_recv.at[4], at_x(right)))
    arrived(q.at[2, hi, :], q_send.at[1], q_recv.at[1], partner)
    sent.append(send(q.at[2, hi, :], q.at[3, hi, :], q_send.at[5], q_recv.at[5], at_x(left)))

    for n in range(NPART):
        cols = pl.ds(n * PART, PART)
        arrived(e1r.at[:, cols], e_send.at[n], e_recv.at[n], partner)
        for j in range(NC):
            rows = slice(j * HALF, (j + 1) * HALF)
            both = keep[rows, n * PART : (n + 1) * PART] + e1r[rows, n * PART : (n + 1) * PART].astype(F32)
            both = both.astype(BF16)
            rsa[j, :, cols] = both[:QTR]
            for m in range(PART // 128):
                block = n * (PART // 128) + m
                hh, zz = block // NZ, block % NZ
                rsb[zz, hh * TOK + j * QTR : hh * TOK + (j + 1) * QTR, :] = both[
                    QTR:, m * 128 : (m + 1) * 128
                ]

    for d in range(1, NY):
        to = (y + d) % NY
        src = rsa.at[to % NC, :, pl.ds(pl.multiple_of((to // NC) * (D // NH), D // NH), D // NH)]
        sent.append(send(src, ra1.at[d], ra1_send.at[d - 1], ra1_recv.at[d - 1], at_y(to)))
        to = (z + d) % NZ
        sent.append(send(rsb.at[to], rb1.at[d], rb1_send.at[d - 1], rb1_recv.at[d - 1], at_z(to)))

    for d in (1, 3, 2):
        piece = hc.at[place[d], half_win, :]
        arrived(piece, h_send.at[d - 1], h_recv.at[d - 1], partner)
        sent.append(send(piece, piece, hf_send.at[d - 1], hf_recv.at[d - 1], partner))
    hc[0] = win[:, pl.ds(pl.multiple_of(x * COLS, COLS), COLS)]

    def form(slot, first, last, factor_row, label_row):
        def step(i, carry):
            rows = pl.ds(pl.multiple_of(i * 64, 64), 64)
            part = q[slot, rows, :].astype(F32)
            grad = jnp.where(part < 0.0, label_row, -part * factor_row)
            gt[rows, slot * WIN : (slot + 1) * WIN] = grad.astype(BF16)
            return carry

        lax.fori_loop(first // 64, last // 64, step, 0)

    def rows_for(d):
        arrived(scale.at[d], x_send.at[d - 1], x_recv.at[d - 1], partner)
        return unfold(scale[d, 0:2, :]), unfold(scale[d, 2:4, :])

    own = rsa[c, :, pl.ds(pl.multiple_of(h * (D // NH), D // NH), D // NH)].astype(F32)
    for d in range(1, NY):
        arrived(ra1.at[d], ra1_send.at[d - 1], ra1_recv.at[d - 1], partner)
        own = own + ra1[d].astype(F32)
    ra2s[...] = own.astype(BF16)
    for d in range(1, NZ):
        to = (z + d) % NZ
        src = ra2s.at[:, pl.ds(pl.multiple_of(to * 128, 128), 128)]
        sent.append(send(src, ra2.at[d], ra2_send.at[d - 1], ra2_recv.at[d - 1], at_z(to)))
    own = rsb[z].astype(F32)
    for d in range(1, NZ):
        arrived(rb1.at[d], rb1_send.at[d - 1], rb1_recv.at[d - 1], partner)
        own = own + rb1[d].astype(F32)
    rb2s[...] = own.astype(BF16)
    for d in range(1, NY):
        to = (y + d) % NY
        src = rb2s.at[pl.ds(pl.multiple_of((to // NC) * TOK + (to % NC) * QTR, QTR), QTR), :]
        sent.append(send(src, rb2.at[d], rb2_send.at[d - 1], rb2_recv.at[d - 1], at_y(to)))

    for d in (1, 3, 2):
        piece = hc.at[place[d], other_win, :]
        arrived(piece, hf_send.at[d - 1], hf_recv.at[d - 1], partner)
    near = rows_for(1)
    arrived(q.at[1, hi, :], q_send.at[2], q_recv.at[2], partner)
    form(1, 0, ROWS, *near)
    near = rows_for(3)
    arrived(q.at[2, lo, :], q_send.at[3], q_recv.at[3], partner)
    form(2, 0, ROWS, *near)
    acc[...] = jnp.dot(
        gt[:, : 3 * WIN], hc[0:3].reshape(3 * WIN, COLS), preferred_element_type=F32
    )

    own = ra2s[:, pl.ds(pl.multiple_of(z * 128, 128), 128)].astype(F32)
    for d in range(1, NZ):
        arrived(ra2.at[d], ra2_send.at[d - 1], ra2_recv.at[d - 1], partner)
        own = own + ra2[d].astype(F32)
    fin[0, 0:QTR, :] = own.astype(BF16)
    own = rb2s[pl.ds(pl.multiple_of(h * TOK + c * QTR, QTR), QTR), :].astype(F32)
    for d in range(1, NY):
        arrived(rb2.at[d], rb2_send.at[d - 1], rb2_recv.at[d - 1], partner)
        own = own + rb2[d].astype(F32)
    fin[0, QTR:HALF, :] = own.astype(BF16)
    sent.append(send(fin.at[0], fin.at[1], fin_send, fin_recv, partner))

    across = rows_for(2)
    arrived(q.at[3, lo, :], q_send.at[4], q_recv.at[4], partner)
    arrived(q.at[3, hi, :], q_send.at[5], q_recv.at[5], partner)
    form(3, 0, ROWS, *across)
    head[...] = (
        acc[...] + jnp.dot(gt[:, 3 * WIN :], hc[3], preferred_element_type=F32)
    ).astype(BF16)
    store = pltpu.make_async_copy(head, head_hbm, loc_sem.at[1])
    store.start()

    arrived(fin.at[1], fin_send, fin_recv, partner)
    for slot, row in ((0, k), (1, 1 - k)):
        value = fin[slot].astype(F32)
        value = jnp.where(k == 0, value[:, :64], value[:, 64:])
        hg_ref[0, pl.ds(pl.multiple_of(row * HALF, HALF), HALF), :] = value.astype(BF16)
    store.wait()
    for copy in sent:
        copy.wait_send()


def body(*args):
    vmem = pl.BlockSpec(memory_space=pltpu.VMEM)
    hbm = pl.BlockSpec(memory_space=pl.ANY)
    dma = pltpu.SemaphoreType.DMA
    return pl.pallas_call(
        kernel,
        out_shape=(
            jax.ShapeDtypeStruct((1, TOK, D // (NH * NZ * 2)), BF16),
            jax.ShapeDtypeStruct((ROWS, COLS), BF16),
        ),
        in_specs=[vmem, hbm] + [vmem] * 6,
        out_specs=(vmem, hbm),
        scratch_shapes=[
            pltpu.VMEM((ROWS, D), BF16),
            pltpu.VMEM((WIN, D), BF16),
            pltpu.VMEM((NX, WIN, COLS), BF16),
            pltpu.VMEM((ROWS, WIN), F32),
            pltpu.VMEM((NX, ROWS, WIN), BF16),
            pltpu.VMEM((ROWS, NX * WIN), BF16),
            pltpu.VMEM((WIN, ROWS), BF16),
            pltpu.VMEM((WIN // 2, D), F32),
            pltpu.VMEM((WIN // 2, D), BF16),
            pltpu.VMEM((WIN // 2, D), BF16),
            pltpu.VMEM((NC, QTR, D), BF16),
            pltpu.VMEM((NZ, NH * TOK, 128), BF16),
            pltpu.VMEM((NY, QTR, D // NH), BF16),
            pltpu.VMEM((NZ, NH * TOK, 128), BF16),
            pltpu.VMEM((QTR, D // NH), BF16),
            pltpu.VMEM((NH * TOK, 128), BF16),
            pltpu.VMEM((NZ, QTR, 128), BF16),
            pltpu.VMEM((NY, QTR, 128), BF16),
            pltpu.VMEM((2, HALF, 128), BF16),
            pltpu.VMEM((2, 8, 128), F32),
            pltpu.VMEM((NY, 8, 128), F32),
            pltpu.VMEM((NZ, 8, 128), F32),
            pltpu.VMEM((NX, 8, 128), F32),
            pltpu.VMEM((ROWS, COLS), F32),
            pltpu.VMEM((ROWS, COLS), BF16),
            dma((2,)),
            dma((3,)),
            dma((3,)),
            dma((3,)),
            dma((3,)),
            dma((3,)),
            dma((3,)),
            dma((3,)),
            dma((3,)),
            dma((6,)),
            dma((6,)),
            dma,
            dma,
            dma((NY - 1,)),
            dma((NY - 1,)),
            dma((NZ - 1,)),
            dma((NZ - 1,)),
            dma((NX - 1,)),
            dma((NX - 1,)),
            dma((NPART,)),
            dma((NPART,)),
            dma((NY - 1,)),
            dma((NY - 1,)),
            dma((NZ - 1,)),
            dma((NZ - 1,)),
            dma((NZ - 1,)),
            dma((NZ - 1,)),
            dma((NY - 1,)),
            dma((NY - 1,)),
            dma,
            dma,
        ],
        compiler_params=pltpu.CompilerParams(
            collective_id=0, has_side_effects=True, vmem_limit_bytes=48 * 1024 * 1024
        ),
        cost_estimate=pl.CostEstimate(
            flops=6 * WIN * D * ROWS, bytes_accessed=2 * ROWS * (D + COLS), transcendentals=4 * ROWS * WIN
        ),
    )(*args)


def solution(mesh):
    placed = (P("dp", "ctx", None), P(("ctx", "vocab"), None)) + (P("dp", None),) * 6
    return jax.shard_map(
        body,
        mesh=mesh,
        in_specs=placed,
        out_specs=(P("dp", "ctx", "vocab"), P(("ctx", "vocab"), "dp")),
        check_vma=False,
    )
```

time: 1430 us -> 65.5 us (0.05)
  the two profiles are of different devices: /device:TPU:54 before, /device:TPU:1 now
where the time goes in v1:
time: 65.5 us; the launch traced here: 65.3 us
  Pallas kernels  56.1 us (86%)
  local copies, waits for them, and re-layouts  8.56 us (13%)
  between operations  0.66 us (1%)
    pallas_call x1, Pallas kernels, body(): pl.pallas_call(kernel, out_shape=(jax.ShapeDtypeStruct((1, TOK, D // (NH...  56.1 us
    unnamed x18, local copies, waits for them, and re-layouts  8.56 us

profile of v1, /device:TPU:1, one launch (start us, length us, event | category | flops | bytes accessed | tf_op | source)
XLA Modules:
  0.0 65.3 jit_solution(3873561805161112726)
XLA Ops:
  0.6 0.0 copy-start
  0.6 2.0 %copy-done = bf16[896,2048]{1,0:T(8,128)(2,1)S(1)} copy-done((bf16[896,2048]{1,0:T(8,128)(2,1)S(1)}, bf16[896,2048]{1,0:T(8,128)(2,1)}, u32[]{:S(2)}) %copy-start) | copy-done | bytes 3670040
  2.7 0.0 copy-start.1
  2.7 0.9 %copy-done.1 = bf16[1,64,2048]{2,1,0:T(8,128)(2,1)S(1)} copy-done((bf16[1,64,2048]{2,1,0:T(8,128)(2,1)S(1)}, bf16[1,64,2048]{2,1,0:T(8,128)(2,1)}, u32[]{:S(2)}) %copy-start.1) | copy-done | bytes 262168
  3.6 0.0 copy-start.2
  3.6 0.7 %copy-done.2 = s32[1,256]{1,0:T(1,128)S(1)} copy-done((s32[1,256]{1,0:T(1,128)S(1)}, s32[1,256]{1,0:T(1,128)}, u32[]{:S(2)}) %copy-start.2) | copy-done | bytes 1048
  4.3 0.0 copy-start.3
  4.3 0.7 %copy-done.3 = s32[1,256]{1,0:T(1,128)S(1)} copy-done((s32[1,256]{1,0:T(1,128)S(1)}, s32[1,256]{1,0:T(1,128)}, u32[]{:S(2)}) %copy-start.3) | copy-done | bytes 1048
  5.0 0.0 copy-start.4
  5.0 0.7 %copy-done.4 = s32[1,256]{1,0:T(1,128)S(1)} copy-done((s32[1,256]{1,0:T(1,128)S(1)}, s32[1,256]{1,0:T(1,128)}, u32[]{:S(2)}) %copy-start.4) | copy-done | bytes 1048
  5.7 0.0 copy-start.5
  5.7 0.7 %copy-done.5 = f32[1,256]{1,0:T(1,128)S(1)} copy-done((f32[1,256]{1,0:T(1,128)S(1)}, f32[1,256]{1,0:T(1,128)}, u32[]{:S(2)}) %copy-start.5) | copy-done | bytes 1048
  6.3 0.0 copy-start.6
  6.3 0.7 %copy-done.6 = f32[1,256]{1,0:T(1,128)S(1)} copy-done((f32[1,256]{1,0:T(1,128)S(1)}, f32[1,256]{1,0:T(1,128)}, u32[]{:S(2)}) %copy-start.6) | copy-done | bytes 1048
  7.0 0.0 copy-start.7
  7.0 0.7 %copy-done.7 = f32[1,8]{1,0:T(1,128)S(1)} copy-done((f32[1,8]{1,0:T(1,128)S(1)}, f32[1,8]{1,0:T(1,128)}, u32[]{:S(2)}) %copy-start.7) | copy-done | bytes 56
  7.7 56.1 %shard_map.95 = (bf16[1,64,64]{2,1,0:T(8,128)(2,1)S(1)}, bf16[896,512]{1,0:T(8,128)(2,1)S(1)}) custom-call(bf16[1,64,2048]{2,1,0:T(8,128)(2,1)S(1)} %copy-done.1, bf16[896,2048]{1,0:T(8,128)(2,1)S(1)} %copy-done, s32[1,256]{1,0:T(1,128)S(1)} %copy-done.2, s32[1,256]{1,0:T(1,128)S(1)} %copy-done.3, s32[1,256]{1,0:T(1,128)S(1)} %copy-done.4, ...), custom_call_target="tpu_custom_call" | custom-call | flops 2818572288 | bytes 4587520 | tf_op jit(solution)/shard_map/pallas_call | solution.py:425
  63.7 0.6 copy.12
  64.3 0.9 %copy.13 = bf16[896,512]{1,0:T(8,128)(2,1)} copy(bf16[896,512]{1,0:T(8,128)(2,1)S(1)} %get-tuple-element.5) | data formatting | bytes 1835008
Async XLA Ops:
  0.6 2.0 %copy-start = (bf16[896,2048]{1,0:T(8,128)(2,1)S(1)}, bf16[896,2048]{1,0:T(8,128)(2,1)}, u32[]{:S(2)}) copy-start(bf16[896,2048]{1,0:T(8,128)(2,1)} %w_hbm.1) | copy-start | bytes 11010052
  2.7 0.9 %copy-start.1 = (bf16[1,64,2048]{2,1,0:T(8,128)(2,1)S(1)}, bf16[1,64,2048]{2,1,0:T(8,128)(2,1)}, u32[]{:S(2)}) copy-start(bf16[1,64,2048]{2,1,0:T(8,128)(2,1)} %hid_ref.1) | copy-start | bytes 786436
  3.6 0.7 %copy-start.2 = (s32[1,256]{1,0:T(1,128)S(1)}, s32[1,256]{1,0:T(1,128)}, u32[]{:S(2)}) copy-start(s32[1,256]{1,0:T(1,128)} %lab_ref.1) | copy-start | bytes 3076
  4.3 0.7 %copy-start.3 = (s32[1,256]{1,0:T(1,128)S(1)}, s32[1,256]{1,0:T(1,128)}, u32[]{:S(2)}) copy-start(s32[1,256]{1,0:T(1,128)} %mask_ref.1) | copy-start | bytes 3076
  5.0 0.7 %copy-start.4 = (s32[1,256]{1,0:T(1,128)S(1)}, s32[1,256]{1,0:T(1,128)}, u32[]{:S(2)}) copy-start(s32[1,256]{1,0:T(1,128)} %seq_ref.1) | copy-start | bytes 3076
  5.7 0.7 %copy-start.5 = (f32[1,256]{1,0:T(1,128)S(1)}, f32[1,256]{1,0:T(1,128)}, u32[]{:S(2)}) copy-start(f32[1,256]{1,0:T(1,128)} %old_ref.1) | copy-start | bytes 3076
  6.3 0.7 %copy-start.6 = (f32[1,256]{1,0:T(1,128)S(1)}, f32[1,256]{1,0:T(1,128)}, u32[]{:S(2)}) copy-start(f32[1,256]{1,0:T(1,128)} %refp_ref.1) | copy-start | bytes 3076
  7.0 0.7 %copy-start.7 = (f32[1,8]{1,0:T(1,128)S(1)}, f32[1,8]{1,0:T(1,128)}, u32[]{:S(2)}) copy-start(f32[1,8]{1,0:T(1,128)} %adv_ref.1) | copy-start | bytes 100

commit v2 on v1

v2 whole, which is shorter than its diff:
```python
import functools

import jax
import jax.numpy as jnp
from jax import lax
from jax.experimental import pallas as pl
from jax.experimental.pallas import tpu as pltpu
from jax.sharding import PartitionSpec as P

CLIP_LOW = 0.2
CLIP_HIGH = 0.28
DUAL_CLIP = 3.0
KL_COEF = 0.04
KL_CAP = 10.0
LOSS_SCALE = 64.0

MESH = pl.DeviceIdType.MESH
F32 = jnp.float32
BF16 = jnp.bfloat16

NX = 4
NC = 4
NH = 2
NY = NC * NH
NZ = 8
WIN = 256
TOK = WIN // NC
HALF = TOK // 2
QTR = HALF // 2
D = 2048
ROWS = 896
CH = 128
COLS = D // NX
PART = 512
NPART = D // PART
SPLIT = ROWS // 2


def token_weights(logp, mask, seq, old, ref, adv_ref):
    adv = jnp.zeros_like(logp)
    length = jnp.zeros_like(logp)
    for s in range(adv_ref.shape[1]):
        match = (seq == s).astype(F32)
        count = jnp.sum(match, axis=1, keepdims=True)
        adv = adv + match * adv_ref[0:1, s : s + 1]
        length = length + match * count
    ratio = jnp.exp(logp - old)
    low = jnp.where(ratio >= 1.0 - CLIP_LOW, jnp.where(ratio <= DUAL_CLIP, 1.0, 0.0), 0.0)
    active = jnp.where(adv >= 0.0, jnp.where(ratio <= 1.0 + CLIP_HIGH, 1.0, 0.0), low)
    policy = jnp.where(active > 0.0, -adv * ratio, 0.0)
    gap = ref - logp
    exp_gap = jnp.exp(gap)
    penalty = jnp.where(exp_gap - gap - 1.0 < KL_CAP, 1.0 - exp_gap, 0.0)
    return LOSS_SCALE * mask.astype(F32) * (policy + KL_COEF * penalty) / length


def merge(ref, n):
    top = ref[0, 0:2, :]
    for i in range(1, n):
        top = jnp.maximum(top, ref[i, 0:2, :])
    total = jnp.zeros_like(top)
    label = jnp.zeros_like(top)
    for i in range(n):
        total = total + ref[i, 2:4, :] * jnp.exp(ref[i, 0:2, :] - top)
        label = label + ref[i, 4:6, :]
    return top, total, label


def put(ref, slot, top, total, label):
    ref[slot] = jnp.concatenate([top, total, label, jnp.zeros_like(top)], axis=0)


def fold(row):
    return jnp.concatenate([row[:, :128], row[:, 128:]], axis=0)


def unfold(tile):
    return jnp.concatenate([tile[0:1, :], tile[1:2, :]], axis=1)


SEMS = 80


def kernel(
    hid_hbm,
    w_hbm,
    lab_hbm,
    mask_hbm,
    seq_hbm,
    old_hbm,
    refp_hbm,
    adv_hbm,
    hg_ref,
    head_ref,
    w,
    win,
    hc,
    logit,
    q,
    gt,
    g,
    keep,
    e1s,
    e1r,
    rsa,
    rsb,
    ra1,
    rb1,
    ra2s,
    rb2s,
    ra2,
    rb2,
    fin,
    st0,
    st1,
    st2,
    scale,
    acc,
    lab_ref,
    mask_ref,
    seq_ref,
    old_ref,
    refp_ref,
    adv_ref,
    loc_sem,
    send_sems,
    recv_sems,
):
    x = lax.axis_index("dp")
    c = lax.axis_index("ctx")
    v = lax.axis_index("vocab")
    h = v // (NZ * 2)
    z = (v // 2) % NZ
    k = v % 2
    y = h * NC + c

    def at_y(to):
        return (x, to % NC, (to // NC) * (NZ * 2) + z * 2 + k)

    def at_z(to):
        return (x, c, h * (NZ * 2) + to * 2 + k)

    def at_x(to):
        return (to, c, v)

    partner = (x, c, h * (NZ * 2) + z * 2 + (1 - k))

    sent = []
    coming = {}

    def send(name, src, dst, landing, to):
        at = len(sent)
        copy = pltpu.make_async_remote_copy(
            src_ref=src,
            dst_ref=dst,
            send_sem=send_sems.at[at],
            recv_sem=recv_sems.at[at],
            device_id=to,
            device_id_type=MESH,
        )
        copy.start()
        sent.append(copy)
        coming[name] = pltpu.make_async_remote_copy(
            src_ref=landing,
            dst_ref=landing,
            send_sem=send_sems.at[at],
            recv_sem=recv_sems.at[at],
            device_id=to,
            device_id_type=MESH,
        )

    def arrived(name):
        coming.pop(name).wait_recv()

    def drain():
        for name in list(coming):
            arrived(name)
        for copy in sent:
            copy.wait_send()

    block = pl.ds(pl.multiple_of(c * TOK, TOK), TOK)
    load_hid = pltpu.make_async_copy(hid_hbm.at[0], win.at[block, :], loc_sem.at[0])
    load_hid.start()
    load_w = pltpu.make_async_copy(w_hbm, w, loc_sem.at[1])
    load_w.start()
    loads = []
    for i, (src, dst) in enumerate(
        (
            (lab_hbm, lab_ref),
            (mask_hbm, mask_ref),
            (seq_hbm, seq_ref),
            (old_hbm, old_ref),
            (refp_hbm, refp_ref),
            (adv_hbm, adv_ref),
        )
    ):
        loads.append(pltpu.make_async_copy(src, dst, loc_sem.at[2 + i]))
        loads[-1].start()

    barrier = pltpu.get_barrier_semaphore()
    peers = [partner]
    peers += [at_y((y + d) % NY) for d in range(1, NY)]
    peers += [at_z((z + d) % NZ) for d in range(1, NZ)]
    peers += [at_x((x + d) % NX) for d in range(1, NX)]
    for peer in peers:
        pl.semaphore_signal(barrier, inc=1, device_id=peer, device_id_type=MESH)
    pl.semaphore_wait(barrier, len(peers))

    def half_block(number, half):
        return win.at[pl.ds(pl.multiple_of(number * TOK + half * HALF, HALF), HALF), :]

    far = (y + NY + 2 - 4 * k) % NY
    from_block = ((c + NC - 1) % NC, (c + 1) % NC, (c + 2) % NC)
    mine = hid_hbm.at[0, pl.ds(pl.multiple_of(k * HALF, HALF), HALF), :]
    for i, to in enumerate(((y + 1) % NY, (y + NY - 1) % NY, far)):
        send(f"a{i}", mine, half_block(c, k), half_block(from_block[i], k), at_y(to))
    for i in range(3):
        arrived(f"a{i}")
        piece = half_block(from_block[i], k)
        send(f"f{i}", piece, piece, half_block(from_block[i], 1 - k), partner)
    load_hid.wait()
    for i in range(3):
        arrived(f"f{i}")

    half_win = pl.ds(pl.multiple_of(k * (WIN // 2), WIN // 2), WIN // 2)
    other_win = pl.ds(pl.multiple_of((1 - k) * (WIN // 2), WIN // 2), WIN // 2)
    place = {0: 0, 1: 1, 3: 2, 2: 3}
    for d in (1, 3, 2):
        to = (x + d) % NX
        src = win.at[half_win, pl.ds(pl.multiple_of(to * COLS, COLS), COLS)]
        dst = hc.at[place[d], half_win, :]
        send(f"h{d}", src, dst, dst, at_x(to))

    load_w.wait()
    for load in loads:
        load.wait()
    logit[...] = lax.dot_general(
        w[...], win[...], (((1,), (1,)), ((), ())), preferred_element_type=F32
    )
    base = (c * (NH * NZ * 2) + v) * ROWS
    local_label = lab_ref[...] - base

    def hit(i):
        rows = lax.broadcasted_iota(jnp.int32, (CH, WIN), 0) + i * CH
        return rows == local_label

    def rows_of(i):
        return pl.ds(pl.multiple_of(i * CH, CH), CH)

    def stat_step(i, carry):
        top, label = carry
        part = logit[rows_of(i), :]
        top = jnp.maximum(top, jnp.max(part, axis=0, keepdims=True))
        label = label + jnp.sum(jnp.where(hit(i), part, 0.0), axis=0, keepdims=True)
        return top, label

    top, label = lax.fori_loop(
        0, ROWS // CH, stat_step, (jnp.full((1, WIN), -jnp.inf, F32), jnp.zeros((1, WIN), F32))
    )

    def exp_step(i, total):
        part = jnp.exp(logit[rows_of(i), :] - top)
        q[0, rows_of(i), :] = jnp.where(hit(i), -1.0, part).astype(BF16)
        return total + jnp.sum(part, axis=0, keepdims=True)

    total = lax.fori_loop(0, ROWS // CH, exp_step, jnp.zeros((1, WIN), F32))

    put(st0, k, fold(top), fold(total), fold(label))
    send("c", st0.at[k], st0.at[k], st0.at[1 - k], partner)

    right, left = (x + 1) % NX, (x + NX - 1) % NX
    lo, hi = pl.ds(0, SPLIT), pl.ds(SPLIT, SPLIT)
    send("q1lo", q.at[0, lo, :], q.at[1, lo, :], q.at[1, lo, :], at_x(right))
    send("q2hi", q.at[0, hi, :], q.at[2, hi, :], q.at[2, hi, :], at_x(left))
    send("q1hi", q.at[0, hi, :], q.at[1, hi, :], q.at[1, hi, :], at_x(right))
    send("q2lo", q.at[0, lo, :], q.at[2, lo, :], q.at[2, lo, :], at_x(left))
    arrived("c")
    put(st1, y, *merge(st0, 2))
    for d in range(1, NY):
        send(f"cy{d}", st1.at[y], st1.at[y], st1.at[(y + NY - d) % NY], at_y((y + d) % NY))
    for d in range(1, NY):
        arrived(f"cy{d}")
    put(st2, z, *merge(st1, NY))
    for d in range(1, NZ):
        send(f"cz{d}", st2.at[z], st2.at[z], st2.at[(z + NZ - d) % NZ], at_z((z + d) % NZ))
    for d in range(1, NZ):
        arrived(f"cz{d}")
    all_top, all_total, all_label = merge(st2, NZ)
    log_total = unfold(all_top + jnp.log(all_total))
    logp = unfold(all_label) - log_total
    coeff = token_weights(
        logp, mask_ref[...], seq_ref[...], old_ref[...], refp_ref[...], adv_ref
    )

    factor = coeff * jnp.exp(top - log_total)
    label_grad = coeff * (1.0 - jnp.exp(logp))
    put(scale, 0, fold(factor), fold(label_grad), fold(label_grad))
    for d in (1, 3, 2):
        send(f"x{d}", scale.at[0], scale.at[d], scale.at[d], at_x((x + d) % NX))

    def grad_step(i, carry):
        grad = coeff * (hit(i).astype(F32) - jnp.exp(logit[rows_of(i), :] - log_total))
        gt[rows_of(i), 0:WIN] = grad.astype(BF16)
        turned = grad.T.astype(BF16)
        for j in range(NC):
            for half in range(2):
                row = j * HALF + (WIN // 2) * (k if half else 1 - k)
                start = j * TOK + half * HALF
                g[pl.ds(pl.multiple_of(row, HALF), HALF), rows_of(i)] = turned[start : start + HALF]
        return carry

    lax.fori_loop(0, ROWS // CH, grad_step, 0)

    for n in range(NPART):
        cols = pl.ds(n * PART, PART)
        value = jnp.dot(g[...], w[:, n * PART : (n + 1) * PART], preferred_element_type=F32)
        e1s[:, cols] = value[: WIN // 2].astype(BF16)
        keep[:, cols] = value[WIN // 2 :]
        send(f"e{n}", e1s.at[:, cols], e1r.at[:, cols], e1r.at[:, cols], partner)
    arrived("q1lo")
    send("q3lo", q.at[1, lo, :], q.at[3, lo, :], q.at[3, lo, :], at_x(right))
    arrived("q2hi")
    send("q3hi", q.at[2, hi, :], q.at[3, hi, :], q.at[3, hi, :], at_x(left))

    for n in range(NPART):
        cols = pl.ds(n * PART, PART)
        arrived(f"e{n}")
        for j in range(NC):
            rows = slice(j * HALF, (j + 1) * HALF)
            both = keep[rows, n * PART : (n + 1) * PART] + e1r[rows, n * PART : (n + 1) * PART].astype(F32)
            both = both.astype(BF16)
            rsa[j, :, cols] = both[:QTR]
            for m in range(PART // 128):
                block = n * (PART // 128) + m
                hh, zz = block // NZ, block % NZ
                rsb[zz, hh * TOK + j * QTR : hh * TOK + (j + 1) * QTR, :] = both[
                    QTR:, m * 128 : (m + 1) * 128
                ]

    for d in range(1, NY):
        to = (y + d) % NY
        src = rsa.at[to % NC, :, pl.ds(pl.multiple_of((to // NC) * (D // NH), D // NH), D // NH)]
        send(f"ya{d}", src, ra1.at[d], ra1.at[d], at_y(to))
        to = (z + d) % NZ
        send(f"zb{d}", rsb.at[to], rb1.at[d], rb1.at[d], at_z(to))

    for d in (1, 3, 2):
        arrived(f"h{d}")
        piece = hc.at[place[d], half_win, :]
        send(f"g{d}", piece, piece, hc.at[place[d], other_win, :], partner)
    hc[0] = win[:, pl.ds(pl.multiple_of(x * COLS, COLS), COLS)]

    def form(slot, first, last, factor_row, label_row):
        def step(i, carry):
            rows = pl.ds(pl.multiple_of(i * 64, 64), 64)
            part = q[slot, rows, :].astype(F32)
            grad = jnp.where(part < 0.0, label_row, -part * factor_row)
            gt[rows, slot * WIN : (slot + 1) * WIN] = grad.astype(BF16)
            return carry

        lax.fori_loop(first // 64, last // 64, step, 0)

    def rows_for(d):
        arrived(f"x{d}")
        return unfold(scale[d, 0:2, :]), unfold(scale[d, 2:4, :])

    own = rsa[c, :, pl.ds(pl.multiple_of(h * (D // NH), D // NH), D // NH)].astype(F32)
    for d in range(1, NY):
        arrived(f"ya{d}")
        own = own + ra1[d].astype(F32)
    ra2s[...] = own
    for d in range(1, NZ):
        to = (z + d) % NZ
        src = ra2s.at[:, pl.ds(pl.multiple_of(to * 128, 128), 128)]
        send(f"za{d}", src, ra2.at[d], ra2.at[d], at_z(to))
    own = rsb[z].astype(F32)
    for d in range(1, NZ):
        arrived(f"zb{d}")
        own = own + rb1[d].astype(F32)
    rb2s[...] = own
    for d in range(1, NY):
        to = (y + d) % NY
        src = rb2s.at[pl.ds(pl.multiple_of((to // NC) * TOK + (to % NC) * QTR, QTR), QTR), :]
        send(f"yb{d}", src, rb2.at[d], rb2.at[d], at_y(to))
    for d in (1, 3, 2):
        arrived(f"g{d}")
    near = rows_for(1)
    arrived("q1hi")
    form(1, 0, ROWS, *near)
    near = rows_for(3)
    arrived("q2lo")
    form(2, 0, ROWS, *near)
    acc[...] = jnp.dot(
        gt[:, : 3 * WIN], hc[0:3].reshape(3 * WIN, COLS), preferred_element_type=F32
    )
    own = ra2s[:, pl.ds(pl.multiple_of(z * 128, 128), 128)]
    for d in range(1, NZ):
        arrived(f"za{d}")
        own = own + ra2[d]
    fin[0, 0:QTR, :] = own.astype(BF16)
    own = rb2s[pl.ds(pl.multiple_of(h * TOK + c * QTR, QTR), QTR), :]
    for d in range(1, NY):
        arrived(f"yb{d}")
        own = own + rb2[d]
    fin[0, QTR:HALF, :] = own.astype(BF16)
    send("fin", fin.at[0], fin.at[1], fin.at[1], partner)
    across = rows_for(2)
    arrived("q3lo")
    arrived("q3hi")
    form(3, 0, ROWS, *across)
    head_ref[...] = (
        acc[...] + jnp.dot(gt[:, 3 * WIN :], hc[3], preferred_element_type=F32)
    ).astype(BF16)

    arrived("fin")
    for slot, row in ((0, k), (1, 1 - k)):
        value = fin[slot].astype(F32)
        value = jnp.where(k == 0, value[:, :64], value[:, 64:])
        hg_ref[0, pl.ds(pl.multiple_of(row * HALF, HALF), HALF), :] = value.astype(BF16)
    drain()


def body(*args):
    vmem = pl.BlockSpec(memory_space=pltpu.VMEM)
    hbm = pl.BlockSpec(memory_space=pltpu.HBM)
    dma = pltpu.SemaphoreType.DMA
    return pl.pallas_call(
        kernel,
        out_shape=(
            jax.ShapeDtypeStruct((1, TOK, D // (NH * NZ * 2)), BF16),
            jax.ShapeDtypeStruct((ROWS, COLS), BF16),
        ),
        in_specs=[hbm] * 8,
        out_specs=(vmem, vmem),
        scratch_shapes=[
            pltpu.VMEM((ROWS, D), BF16),
            pltpu.VMEM((WIN, D), BF16),
            pltpu.VMEM((NX, WIN, COLS), BF16),
            pltpu.VMEM((ROWS, WIN), F32),
            pltpu.VMEM((NX, ROWS, WIN), BF16),
            pltpu.VMEM((ROWS, NX * WIN), BF16),
            pltpu.VMEM((WIN, ROWS), BF16),
            pltpu.VMEM((WIN // 2, D), F32),
            pltpu.VMEM((WIN // 2, D), BF16),
            pltpu.VMEM((WIN // 2, D), BF16),
            pltpu.VMEM((NC, QTR, D), BF16),
            pltpu.VMEM((NZ, NH * TOK, 128), BF16),
            pltpu.VMEM((NY, QTR, D // NH), BF16),
            pltpu.VMEM((NZ, NH * TOK, 128), BF16),
            pltpu.VMEM((QTR, D // NH), F32),
            pltpu.VMEM((NH * TOK, 128), F32),
            pltpu.VMEM((NZ, QTR, 128), F32),
            pltpu.VMEM((NY, QTR, 128), F32),
            pltpu.VMEM((2, HALF, 128), BF16),
            pltpu.VMEM((2, 8, 128), F32),
            pltpu.VMEM((NY, 8, 128), F32),
            pltpu.VMEM((NZ, 8, 128), F32),
            pltpu.VMEM((NX, 8, 128), F32),
            pltpu.VMEM((ROWS, COLS), F32),
            pltpu.VMEM((1, WIN), jnp.int32),
            pltpu.VMEM((1, WIN), jnp.int32),
            pltpu.VMEM((1, WIN), jnp.int32),
            pltpu.VMEM((1, WIN), F32),
            pltpu.VMEM((1, WIN), F32),
            pltpu.VMEM((1, 8), F32),
            dma((8,)),
            dma((SEMS,)),
            dma((SEMS,)),
        ],
        compiler_params=pltpu.CompilerParams(
            collective_id=0, has_side_effects=True, vmem_limit_bytes=60 * 1024 * 1024
        ),
        cost_estimate=pl.CostEstimate(
            flops=6 * WIN * D * ROWS, bytes_accessed=2 * ROWS * (D + COLS), transcendentals=4 * ROWS * WIN
        ),
    )(*args)


def solution(mesh):
    placed = (P("dp", "ctx", None), P(("ctx", "vocab"), None)) + (P("dp", None),) * 6
    return jax.shard_map(
        body,
        mesh=mesh,
        in_specs=placed,
        out_specs=(P("dp", "ctx", "vocab"), P(("ctx", "vocab"), "dp")),
        check_vma=False,
    )
```

time: 65.5 us -> 61.8 us (0.944)
  local copies, waits for them, and re-layouts: 8.56 us -> 3.48 us
  Pallas kernels: 56.1 us -> 57.5 us
    unnamed x18 -> x2, local copies, waits for them, and re-layouts: 8.56 us -> 3.48 us
    pallas_call x1, Pallas kernels: 56.1 us -> 57.5 us  [body(): pl.pallas_call(kernel, out_shape=(jax.ShapeDtypeStruct((1, TOK, D // (NH...]
where the time goes in v2:
time: 61.8 us; the launch traced here: 61.6 us
  Pallas kernels  57.5 us (93%)
  local copies, waits for them, and re-layouts  3.48 us (6%)
  between operations  0.64 us (1%)
    pallas_call x1, Pallas kernels, body(): pl.pallas_call(kernel, out_shape=(jax.ShapeDtypeStruct((1, TOK, D // (NH...  57.5 us
    unnamed x2, local copies, waits for them, and re-layouts  3.48 us

profile of v2, /device:TPU:1, one launch (start us, length us, event | category | flops | bytes accessed | tf_op | source)
XLA Modules:
  0.0 61.6 jit_solution(4027303310406655365)
XLA Ops:
  0.6 57.5 %shard_map.95 = (bf16[1,64,64]{2,1,0:T(8,128)(2,1)}, bf16[896,512]{1,0:T(8,128)(2,1)}) custom-call(bf16[1,64,2048]{2,1,0:T(8,128)(2,1)} %hid_hbm.1, bf16[896,2048]{1,0:T(8,128)(2,1)} %w_hbm.1, s32[1,256]{1,0:T(1,128)} %lab_hbm.1, s32[1,256]{1,0:T(1,128)} %mask_hbm.1, s32[1,256]{1,0:T(1,128)} %seq_hbm.1, f32[1,256]{1,0:T(1,128)} %old_hbm.1, ...), custom_call_target="tpu_custom_call" | custom-call | flops 2818572288 | bytes 4587520 | tf_op jit(solution)/shard_map/pallas_call | solution.py:427
  58.1 1.3 %copy.12 = bf16[1,64,64]{2,1,0:T(8,128)(2,1)} copy(bf16[1,64,64]{2,1,0:T(8,128)(2,1)} %get-tuple-element.4) | data formatting | bytes 16384
  59.4 2.2 %copy.13 = bf16[896,512]{1,0:T(8,128)(2,1)} copy(bf16[896,512]{1,0:T(8,128)(2,1)} %get-tuple-element.5) | data formatting | bytes 1835008

commit v3 on v2

v3 whole, which is shorter than its diff:
```python
import functools

import jax
import jax.numpy as jnp
from jax import lax
from jax.experimental import pallas as pl
from jax.experimental.pallas import tpu as pltpu
from jax.sharding import PartitionSpec as P

CLIP_LOW = 0.2
CLIP_HIGH = 0.28
DUAL_CLIP = 3.0
KL_COEF = 0.04
KL_CAP = 10.0
LOSS_SCALE = 64.0

MESH = pl.DeviceIdType.MESH
F32 = jnp.float32
BF16 = jnp.bfloat16

NX = 4
NC = 4
NH = 2
NY = NC * NH
NZ = 8
WIN = 256
TOK = WIN // NC
HALF = TOK // 2
QTR = HALF // 2
D = 2048
ROWS = 896
CH = 128
COLS = D // NX
PART = 512
NPART = D // PART
SPLIT = ROWS // 2


def token_weights(logp, mask, seq, old, ref, adv_ref):
    adv = jnp.zeros_like(logp)
    length = jnp.zeros_like(logp)
    for s in range(adv_ref.shape[1]):
        match = (seq == s).astype(F32)
        count = jnp.sum(match, axis=1, keepdims=True)
        adv = adv + match * adv_ref[0:1, s : s + 1]
        length = length + match * count
    ratio = jnp.exp(logp - old)
    low = jnp.where(ratio >= 1.0 - CLIP_LOW, jnp.where(ratio <= DUAL_CLIP, 1.0, 0.0), 0.0)
    active = jnp.where(adv >= 0.0, jnp.where(ratio <= 1.0 + CLIP_HIGH, 1.0, 0.0), low)
    policy = jnp.where(active > 0.0, -adv * ratio, 0.0)
    gap = ref - logp
    exp_gap = jnp.exp(gap)
    penalty = jnp.where(exp_gap - gap - 1.0 < KL_CAP, 1.0 - exp_gap, 0.0)
    return LOSS_SCALE * mask.astype(F32) * (policy + KL_COEF * penalty) / length


def merge(ref, n):
    top = ref[0, 0:2, :]
    for i in range(1, n):
        top = jnp.maximum(top, ref[i, 0:2, :])
    total = jnp.zeros_like(top)
    label = jnp.zeros_like(top)
    for i in range(n):
        total = total + ref[i, 2:4, :] * jnp.exp(ref[i, 0:2, :] - top)
        label = label + ref[i, 4:6, :]
    return top, total, label


def turn(rows, out):
    rows = list(rows) + [jnp.zeros_like(rows[0])] * (8 - len(rows))
    out[...] = jnp.concatenate(rows, axis=0).T


def put(ref, slot, top, total, label):
    ref[slot] = jnp.concatenate([top, total, label, jnp.zeros_like(top)], axis=0)


def fold(row):
    return jnp.concatenate([row[:, :128], row[:, 128:]], axis=0)


def unfold(tile):
    return jnp.concatenate([tile[0:1, :], tile[1:2, :]], axis=1)


SEMS = 140


def kernel(
    hid_hbm,
    w_hbm,
    lab_hbm,
    mask_hbm,
    seq_hbm,
    old_hbm,
    refp_hbm,
    adv_hbm,
    hg_ref,
    head_ref,
    w,
    win,
    hc,
    logit,
    q,
    gt,
    g,
    keep,
    e1s,
    e1r,
    keepl,
    els,
    elr,
    rsa,
    rsb,
    rsl,
    ra1,
    rb1,
    rl1,
    ra2s,
    rb2s,
    rl2s,
    ra2,
    rb2,
    rl2,
    fin,
    st0,
    sty,
    stz,
    styz,
    stzy,
    scale,
    col0,
    col1a,
    col1b,
    col2a,
    col2b,
    coll,
    acc,
    lab_ref,
    mask_ref,
    seq_ref,
    old_ref,
    refp_ref,
    adv_ref,
    loc_sem,
    send_sems,
    recv_sems,
):
    x = lax.axis_index("dp")
    c = lax.axis_index("ctx")
    v = lax.axis_index("vocab")
    h = v // (NZ * 2)
    z = (v // 2) % NZ
    k = v % 2
    y = h * NC + c

    def at_y(to):
        return (x, to % NC, (to // NC) * (NZ * 2) + z * 2 + k)

    def at_z(to):
        return (x, c, h * (NZ * 2) + to * 2 + k)

    def at_x(to):
        return (to, c, v)

    partner = (x, c, h * (NZ * 2) + z * 2 + (1 - k))

    sent = []
    coming = {}

    def send(name, src, dst, landing, to):
        at = len(sent)
        copy = pltpu.make_async_remote_copy(
            src_ref=src,
            dst_ref=dst,
            send_sem=send_sems.at[at],
            recv_sem=recv_sems.at[at],
            device_id=to,
            device_id_type=MESH,
        )
        copy.start()
        sent.append(copy)
        coming[name] = pltpu.make_async_remote_copy(
            src_ref=landing,
            dst_ref=landing,
            send_sem=send_sems.at[at],
            recv_sem=recv_sems.at[at],
            device_id=to,
            device_id_type=MESH,
        )

    def arrived(name):
        coming.pop(name).wait_recv()

    def drain():
        for name in list(coming):
            arrived(name)
        for copy in sent:
            copy.wait_send()

    block = pl.ds(pl.multiple_of(c * TOK, TOK), TOK)
    load_hid = pltpu.make_async_copy(hid_hbm.at[0], win.at[block, :], loc_sem.at[0])
    load_hid.start()
    load_w = pltpu.make_async_copy(w_hbm, w, loc_sem.at[1])
    load_w.start()
    loads = []
    for i, (src, dst) in enumerate(
        (
            (lab_hbm, lab_ref),
            (mask_hbm, mask_ref),
            (seq_hbm, seq_ref),
            (old_hbm, old_ref),
            (refp_hbm, refp_ref),
            (adv_hbm, adv_ref),
        )
    ):
        loads.append(pltpu.make_async_copy(src, dst, loc_sem.at[2 + i]))
        loads[-1].start()

    barrier = pltpu.get_barrier_semaphore()
    peers = [partner]
    peers += [at_y((y + d) % NY) for d in range(1, NY)]
    peers += [at_z((z + d) % NZ) for d in range(1, NZ)]
    peers += [at_x((x + d) % NX) for d in range(1, NX)]
    for peer in peers:
        pl.semaphore_signal(barrier, inc=1, device_id=peer, device_id_type=MESH)
    pl.semaphore_wait(barrier, len(peers))

    def half_rows(number, half):
        return pl.ds(pl.multiple_of(number * TOK + half * HALF, HALF), HALF)

    def rows_of(i):
        return pl.ds(pl.multiple_of(i * CH, CH), CH)

    place = {0: 0, 1: 1, 3: 2, 2: 3}
    right, left = (x + 1) % NX, (x + NX - 1) % NX

    far = (y + NY + 2 - 4 * k) % NY
    from_block = ((c + NC - 1) % NC, (c + 1) % NC, (c + 2) % NC)
    mine = hid_hbm.at[0, pl.ds(pl.multiple_of(k * HALF, HALF), HALF), :]
    for i, to in enumerate(((y + 1) % NY, (y + NY - 1) % NY, far)):
        send(
            f"a{i}", mine, win.at[half_rows(c, k), :], win.at[half_rows(from_block[i], k), :], at_y(to)
        )

    def spread_columns(i, number, src):
        for d in (1, 3, 2):
            to = (x + d) % NX
            part = src.at[:, pl.ds(pl.multiple_of(to * COLS, COLS), COLS)]
            dst = hc.at[place[d], half_rows(number, k), :]
            send(f"h{i}{d}", part, dst, dst, at_x(to))

    spread_columns(3, c, mine)

    load_w.wait()
    for load in loads:
        load.wait()
    base = (c * (NH * NZ * 2) + v) * ROWS
    local_label = lab_ref[...] - base

    def hit(i):
        rows = lax.broadcasted_iota(jnp.int32, (CH, WIN), 0) + i * CH
        return rows == local_label

    def put_turned(i, value):
        turned = value.T.astype(BF16)
        for j in range(NC):
            for half in range(2):
                row = j * HALF + (WIN // 2) * (1 - k if half == 0 else k)
                start = j * TOK + half * HALF
                g[pl.ds(pl.multiple_of(row, HALF), HALF), rows_of(i)] = turned[start : start + HALF]

    def label_step(i, carry):
        put_turned(i, hit(i).astype(F32))
        return carry

    lax.fori_loop(0, ROWS // CH, label_step, 0)
    for n in range(NPART):
        cols = pl.ds(n * PART, PART)
        value = jnp.dot(g[...], w[:, n * PART : (n + 1) * PART], preferred_element_type=F32)
        els[:, cols] = value[: WIN // 2].astype(BF16)
        keepl[:, cols] = value[WIN // 2 :].astype(BF16)
    send("l", els, elr, elr, partner)
    arrived("l")
    for j in range(NC):
        rows = slice(j * HALF, (j + 1) * HALF)
        both = (keepl[rows, :].astype(F32) + elr[rows, :].astype(F32)).astype(BF16)
        for m in range(D // 128):
            hh, zz = m // NZ, m % NZ
            rsl[zz, hh * (NC * HALF) + j * HALF : hh * (NC * HALF) + (j + 1) * HALF, :] = both[
                :, m * 128 : (m + 1) * 128
            ]
    for d in range(1, NZ):
        to = (z + d) % NZ
        send(f"zl{d}", rsl.at[to], rl1.at[d], rl1.at[d], at_z(to))

    for i in range(3):
        arrived(f"a{i}")
        piece = win.at[half_rows(from_block[i], k), :]
        send(f"f{i}", piece, piece, win.at[half_rows(from_block[i], 1 - k), :], partner)
        spread_columns(i, from_block[i], piece)
    load_hid.wait()
    for i in range(3):
        arrived(f"f{i}")
    logit[...] = lax.dot_general(
        w[...], win[...], (((1,), (1,)), ((), ())), preferred_element_type=F32
    )

    def stat_step(i, carry):
        top, label = carry
        part = logit[rows_of(i), :]
        here = hit(i)
        top = jnp.maximum(top, jnp.max(jnp.where(here, -jnp.inf, part), axis=0, keepdims=True))
        label = label + jnp.sum(jnp.where(here, part, 0.0), axis=0, keepdims=True)
        return top, label

    top, label = lax.fori_loop(
        0, ROWS // CH, stat_step, (jnp.full((1, WIN), -jnp.inf, F32), jnp.zeros((1, WIN), F32))
    )

    def exp_step(i, total):
        here = hit(i)
        part = jnp.where(here, 0.0, jnp.exp(logit[rows_of(i), :] - top))
        q[0, rows_of(i), :] = jnp.where(here, -1.0, part).astype(BF16)
        put_turned(i, part)
        return total + jnp.sum(part, axis=0, keepdims=True)

    total = lax.fori_loop(0, ROWS // CH, exp_step, jnp.zeros((1, WIN), F32))
    put(st0, k, fold(top), fold(total), fold(label))
    send("c", st0.at[k], st0.at[k], st0.at[1 - k], partner)

    lo, hi = pl.ds(0, SPLIT), pl.ds(SPLIT, SPLIT)
    send("q1lo", q.at[0, lo, :], q.at[1, lo, :], q.at[1, lo, :], at_x(right))
    send("q2hi", q.at[0, hi, :], q.at[2, hi, :], q.at[2, hi, :], at_x(left))
    for n in range(NPART):
        cols = pl.ds(n * PART, PART)
        value = jnp.dot(g[...], w[:, n * PART : (n + 1) * PART], preferred_element_type=F32)
        e1s[:, cols] = value[: WIN // 2].astype(BF16)
        keep[:, cols] = value[WIN // 2 :]
        send(f"e{n}", e1s.at[:, cols], e1r.at[:, cols], e1r.at[:, cols], partner)

    arrived("c")
    pair = merge(st0, 2)
    put(sty, y, *pair)
    put(stz, z, *pair)
    for d in range(1, NY):
        send(f"cy{d}", sty.at[y], sty.at[y], sty.at[(y + NY - d) % NY], at_y((y + d) % NY))
    for d in range(1, NZ):
        send(f"cz{d}", stz.at[z], stz.at[z], stz.at[(z + NZ - d) % NZ], at_z((z + d) % NZ))

    def relative(ref, slot, norm):
        return unfold(jnp.exp(ref[slot, 0:2, :] - norm))

    turn([relative(st0, k, pair[0]), relative(st0, 1 - k, pair[0])], col0)
    for n in range(NPART):
        cols = pl.ds(n * PART, PART)
        arrived(f"e{n}")
        for j in range(NC):
            rows = slice(j * HALF, (j + 1) * HALF)
            factors = col0[half_rows(j, k), :]
            both = keep[rows, n * PART : (n + 1) * PART] * factors[:, 0:1]
            both = both + e1r[rows, n * PART : (n + 1) * PART].astype(F32) * factors[:, 1:2]
            both = both.astype(BF16)
            rsa[j, :, cols] = both[:QTR]
            for m in range(PART // 128):
                block = n * (PART // 128) + m
                hh, zz = block // NZ, block % NZ
                rsb[zz, hh * TOK + j * QTR : hh * TOK + (j + 1) * QTR, :] = both[
                    QTR:, m * 128 : (m + 1) * 128
                ]

    for d in range(1, NY):
        to = (y + d) % NY
        src = rsa.at[to % NC, :, pl.ds(pl.multiple_of((to // NC) * (D // NH), D // NH), D // NH)]
        send(f"ya{d}", src, ra1.at[d], ra1.at[d], at_y(to))
        to = (z + d) % NZ
        send(f"zb{d}", rsb.at[to], rb1.at[d], rb1.at[d], at_z(to))
    send("q1hi", q.at[0, hi, :], q.at[1, hi, :], q.at[1, hi, :], at_x(right))
    send("q2lo", q.at[0, lo, :], q.at[2, lo, :], q.at[2, lo, :], at_x(left))
    own = rsl[z].astype(F32)
    for d in range(1, NZ):
        arrived(f"zl{d}")
        own = own + rl1[d].astype(F32)
    rl2s[...] = own.astype(BF16)
    for d in range(1, NY):
        to = (y + d) % NY
        src = rl2s.at[pl.ds(pl.multiple_of((to // NC) * (NC * HALF) + (to % NC) * HALF, HALF), HALF), :]
        send(f"yl{d}", src, rl2.at[d], rl2.at[d], at_y(to))

    for i, number in ((3, c), (0, from_block[0]), (1, from_block[1]), (2, from_block[2])):
        for d in (1, 3, 2):
            arrived(f"h{i}{d}")
            piece = hc.at[place[d], half_rows(number, k), :]
            send(f"g{i}{d}", piece, piece, hc.at[place[d], half_rows(number, 1 - k), :], partner)
    hc[0] = win[:, pl.ds(pl.multiple_of(x * COLS, COLS), COLS)]

    for d in range(1, NY):
        arrived(f"cy{d}")
    ring_y = merge(sty, NY)
    put(styz, z, *ring_y)
    for d in range(1, NZ):
        send(f"cyz{d}", styz.at[z], styz.at[z], styz.at[(z + NZ - d) % NZ], at_z((z + d) % NZ))
    for d in range(1, NZ):
        arrived(f"cz{d}")
    ring_z = merge(stz, NZ)
    put(stzy, y, *ring_z)
    for d in range(1, NY):
        send(f"czy{d}", stzy.at[y], stzy.at[y], stzy.at[(y + NY - d) % NY], at_y((y + d) % NY))
    turn([relative(sty, (y + NY - d) % NY, ring_y[0]) for d in range(NY)], col1a)
    turn([relative(stz, (z + NZ - d) % NZ, ring_z[0]) for d in range(NZ)], col1b)

    arrived("q1lo")
    send("q3lo", q.at[1, lo, :], q.at[3, lo, :], q.at[3, lo, :], at_x(right))
    arrived("q2hi")
    send("q3hi", q.at[2, hi, :], q.at[3, hi, :], q.at[3, hi, :], at_x(left))
    rows_a = pl.ds(pl.multiple_of(c * TOK + k * HALF, QTR), QTR)
    rows_b = pl.ds(pl.multiple_of(c * TOK + k * HALF + QTR, QTR), QTR)
    factors = col1a[rows_a, :]
    own = rsa[c, :, pl.ds(pl.multiple_of(h * (D // NH), D // NH), D // NH)].astype(F32) * factors[:, 0:1]
    for d in range(1, NY):
        arrived(f"ya{d}")
        own = own + ra1[d].astype(F32) * factors[:, d : d + 1]
    ra2s[...] = own
    for d in range(1, NZ):
        to = (z + d) % NZ
        src = ra2s.at[:, pl.ds(pl.multiple_of(to * 128, 128), 128)]
        send(f"za{d}", src, ra2.at[d], ra2.at[d], at_z(to))
    factors = [
        col1b[pl.ds(pl.multiple_of(j * TOK + k * HALF + QTR, QTR), QTR), :] for j in range(NC)
    ]
    factors = jnp.concatenate(factors + factors, axis=0)
    own = rsb[z].astype(F32) * factors[:, 0:1]
    for d in range(1, NZ):
        arrived(f"zb{d}")
        own = own + rb1[d].astype(F32) * factors[:, d : d + 1]
    rb2s[...] = own
    for d in range(1, NY):
        to = (y + d) % NY
        src = rb2s.at[pl.ds(pl.multiple_of((to // NC) * TOK + (to % NC) * QTR, QTR), QTR), :]
        send(f"yb{d}", src, rb2.at[d], rb2.at[d], at_y(to))
    for d in range(1, NZ):
        arrived(f"cyz{d}")
    all_top, all_rest, all_label = merge(styz, NZ)
    peak = jnp.maximum(all_top, all_label)
    rest = all_rest * jnp.exp(all_top - peak)
    whole = rest + jnp.exp(all_label - peak)
    log_total = peak + jnp.log(whole)
    row_total = unfold(log_total)
    coeff = token_weights(
        unfold(all_label - log_total), mask_ref[...], seq_ref[...], old_ref[...], refp_ref[...], adv_ref
    )
    factor = coeff * jnp.exp(top - row_total)
    label_grad = coeff * unfold(rest / whole)
    put(scale, 0, fold(factor), fold(label_grad), fold(label_grad))
    for d in (1, 3, 2):
        send(f"x{d}", scale.at[0], scale.at[d], scale.at[d], at_x((x + d) % NX))

    def form(slot, factor_row, label_row):
        def step(i, carry):
            part = q[slot, rows_of(i), :].astype(F32)
            grad = jnp.where(part < 0.0, label_row, -part * factor_row)
            gt[rows_of(i), slot * WIN : (slot + 1) * WIN] = grad.astype(BF16)
            return carry

        lax.fori_loop(0, ROWS // CH, step, 0)

    def rows_for(d):
        arrived(f"x{d}")
        return unfold(scale[d, 0:2, :]), unfold(scale[d, 2:4, :])

    form(0, factor, label_grad)
    for d in range(1, NY):
        arrived(f"czy{d}")
    turn([-coeff * relative(styz, (z + NZ - d) % NZ, log_total) for d in range(NZ)], col2a)
    turn([-coeff * relative(stzy, (y + NY - d) % NY, log_total) for d in range(NY)], col2b)
    turn([label_grad], coll)
    own = rl2s[pl.ds(pl.multiple_of(h * (NC * HALF) + c * HALF, HALF), HALF), :].astype(F32)
    for d in range(1, NY):
        arrived(f"yl{d}")
        own = own + rl2[d].astype(F32)
    own_label = own * coll[half_rows(c, k), :][:, 0:1]

    for i in range(4):
        for d in (1, 3, 2):
            arrived(f"g{i}{d}")
    near = rows_for(1)
    arrived("q1hi")
    form(1, *near)
    near = rows_for(3)
    arrived("q2lo")
    form(2, *near)
    acc[...] = jnp.dot(
        gt[:, : 3 * WIN], hc[0:3].reshape(3 * WIN, COLS), preferred_element_type=F32
    )

    factors = col2a[rows_a, :]
    own = own_label[:QTR]
    own = own + ra2s[:, pl.ds(pl.multiple_of(z * 128, 128), 128)] * factors[:, 0:1]
    for d in range(1, NZ):
        arrived(f"za{d}")
        own = own + ra2[d] * factors[:, d : d + 1]
    fin[0, 0:QTR, :] = own.astype(BF16)
    factors = col2b[rows_b, :]
    own = own_label[QTR:]
    own = own + rb2s[pl.ds(pl.multiple_of(h * TOK + c * QTR, QTR), QTR), :] * factors[:, 0:1]
    for d in range(1, NY):
        arrived(f"yb{d}")
        own = own + rb2[d] * factors[:, d : d + 1]
    fin[0, QTR:HALF, :] = own.astype(BF16)
    send("fin", fin.at[0], fin.at[1], fin.at[1], partner)
    across = rows_for(2)
    arrived("q3lo")
    arrived("q3hi")
    form(3, *across)
    head_ref[...] = (
        acc[...] + jnp.dot(gt[:, 3 * WIN :], hc[3], preferred_element_type=F32)
    ).astype(BF16)

    arrived("fin")
    for slot, row in ((0, k), (1, 1 - k)):
        value = fin[slot].astype(F32)
        value = jnp.where(k == 0, value[:, :64], value[:, 64:])
        hg_ref[0, pl.ds(pl.multiple_of(row * HALF, HALF), HALF), :] = value.astype(BF16)
    drain()


def body(*args):
    vmem = pl.BlockSpec(memory_space=pltpu.VMEM)
    hbm = pl.BlockSpec(memory_space=pltpu.HBM)
    dma = pltpu.SemaphoreType.DMA
    args = [pltpu.with_memory_space_constraint(a, pltpu.HBM) for a in args]
    return pl.pallas_call(
        kernel,
        out_shape=(
            pltpu.VMEM((1, TOK, D // (NH * NZ * 2)), BF16),
            pltpu.VMEM((ROWS, COLS), BF16),
        ),
        in_specs=[hbm] * 8,
        out_specs=(vmem, vmem),
        scratch_shapes=[
            pltpu.VMEM((ROWS, D), BF16),
            pltpu.VMEM((WIN, D), BF16),
            pltpu.VMEM((NX, WIN, COLS), BF16),
            pltpu.VMEM((ROWS, WIN), F32),
            pltpu.VMEM((NX, ROWS, WIN), BF16),
            pltpu.VMEM((ROWS, NX * WIN), BF16),
            pltpu.VMEM((WIN, ROWS), BF16),
            pltpu.VMEM((WIN // 2, D), F32),
            pltpu.VMEM((WIN // 2, D), BF16),
            pltpu.VMEM((WIN // 2, D), BF16),
            pltpu.VMEM((WIN // 2, D), BF16),
            pltpu.VMEM((WIN // 2, D), BF16),
            pltpu.VMEM((WIN // 2, D), BF16),
            pltpu.VMEM((NC, QTR, D), BF16),
            pltpu.VMEM((NZ, NH * TOK, 128), BF16),
            pltpu.VMEM((NZ, NH * NC * HALF, 128), BF16),
            pltpu.VMEM((NY, QTR, D // NH), BF16),
            pltpu.VMEM((NZ, NH * TOK, 128), BF16),
            pltpu.VMEM((NZ, NH * NC * HALF, 128), BF16),
            pltpu.VMEM((QTR, D // NH), F32),
            pltpu.VMEM((NH * TOK, 128), F32),
            pltpu.VMEM((NH * NC * HALF, 128), BF16),
            pltpu.VMEM((NZ, QTR, 128), F32),
            pltpu.VMEM((NY, QTR, 128), F32),
            pltpu.VMEM((NY, HALF, 128), BF16),
            pltpu.VMEM((2, HALF, 128), BF16),
            pltpu.VMEM((2, 8, 128), F32),
            pltpu.VMEM((NY, 8, 128), F32),
            pltpu.VMEM((NZ, 8, 128), F32),
            pltpu.VMEM((NZ, 8, 128), F32),
            pltpu.VMEM((NY, 8, 128), F32),
            pltpu.VMEM((NX, 8, 128), F32),
            pltpu.VMEM((WIN, 8), F32),
            pltpu.VMEM((WIN, 8), F32),
            pltpu.VMEM((WIN, 8), F32),
            pltpu.VMEM((WIN, 8), F32),
            pltpu.VMEM((WIN, 8), F32),
            pltpu.VMEM((WIN, 8), F32),
            pltpu.VMEM((ROWS, COLS), F32),
            pltpu.VMEM((1, WIN), jnp.int32),
            pltpu.VMEM((1, WIN), jnp.int32),
            pltpu.VMEM((1, WIN), jnp.int32),
            pltpu.VMEM((1, WIN), F32),
            pltpu.VMEM((1, WIN), F32),
            pltpu.VMEM((1, 8), F32),
            dma((8,)),
            dma((SEMS,)),
            dma((SEMS,)),
        ],
        compiler_params=pltpu.CompilerParams(
            collective_id=0, has_side_effects=True, vmem_limit_bytes=48 * 1024 * 1024
        ),
        cost_estimate=pl.CostEstimate(
            flops=8 * WIN * D * ROWS, bytes_accessed=2 * ROWS * (D + COLS), transcendentals=4 * ROWS * WIN
        ),
    )(*args)


def solution(mesh):
    placed = (P("dp", "ctx", None), P(("ctx", "vocab"), None)) + (P("dp", None),) * 6
    return jax.shard_map(
        body,
        mesh=mesh,
        in_specs=placed,
        out_specs=(P("dp", "ctx", "vocab"), P(("ctx", "vocab"), "dp")),
        check_vma=False,
    )
```

time: 61.8 us -> 52.2 us (0.84)
  Pallas kernels: 57.5 us -> 50 us
  local copies, waits for them, and re-layouts: 3.48 us -> 1.53 us
    pallas_call x1, Pallas kernels: 57.5 us -> 50 us  [body(): pl.pallas_call(kernel, out_shape=(pltpu.VMEM((1, TOK, D // (NH * NZ * 2))...]
    unnamed x2, local copies, waits for them, and re-layouts: 3.48 us -> 1.53 us
where the time goes in v3:
time: 52.2 us; the launch traced here: 52.1 us
  Pallas kernels  50 us (96%)
  local copies, waits for them, and re-layouts  1.53 us (3%)
  between operations  0.64 us (1%)
    pallas_call x1, Pallas kernels, body(): pl.pallas_call(kernel, out_shape=(pltpu.VMEM((1, TOK, D // (NH * NZ * 2))...  50 us
    unnamed x2, local copies, waits for them, and re-layouts  1.53 us

profile of v3, /device:TPU:1, one launch (start us, length us, event | category | flops | bytes accessed | tf_op | source)
XLA Modules:
  0.0 52.1 jit_solution(2945123700018419902)
XLA Ops:
  0.6 50.0 %shard_map.95 = (bf16[1,64,64]{2,1,0:T(8,128)(2,1)S(1)}, bf16[896,512]{1,0:T(8,128)(2,1)S(1)}) custom-call(bf16[1,64,2048]{2,1,0:T(8,128)(2,1)} %hid_hbm.1, bf16[896,2048]{1,0:T(8,128)(2,1)} %w_hbm.1, s32[1,256]{1,0:T(1,128)} %lab_hbm.1, s32[1,256]{1,0:T(1,128)} %mask_hbm.1, s32[1,256]{1,0:T(1,128)} %seq_hbm.1, f32[1,256]{1,0:T(1,128)} %old_hbm.1, ...), custom_call_target="tpu_custom_call" | custom-call | flops 3758096384 | bytes 4587520 | tf_op jit(solution)/shard_map/pallas_call | solution.py:532
  50.6 0.6 %copy.12 = bf16[1,64,64]{2,1,0:T(8,128)(2,1)} copy(bf16[1,64,64]{2,1,0:T(8,128)(2,1)S(1)} %get-tuple-element.2) | data formatting | bytes 16384
  51.2 0.9 %copy.13 = bf16[896,512]{1,0:T(8,128)(2,1)} copy(bf16[896,512]{1,0:T(8,128)(2,1)S(1)} %get-tuple-element.3) | data formatting | bytes 1835008

commit v4 on v3

--- a/solution.py
+++ b/solution.py
@@ -84,6 +84,8 @@
 
 
 SEMS = 140
+BLOCK = 448
+FAR = (4, 3, 5, 2, 6, 1, 7)
 
 
 def kernel(
@@ -135,7 +137,6 @@
     col2a,
     col2b,
     coll,
-    acc,
     lab_ref,
     mask_ref,
     seq_ref,
@@ -167,6 +168,8 @@
 
     sent = []
     coming = {}
+    names = []
+    settled = set()
 
     def send(name, src, dst, landing, to):
         at = len(sent)
@@ -180,6 +183,7 @@
         )
         copy.start()
         sent.append(copy)
+        names.append(name)
         coming[name] = pltpu.make_async_remote_copy(
             src_ref=landing,
             dst_ref=landing,
@@ -195,8 +199,13 @@
     def drain():
         for name in list(coming):
             arrived(name)
-        for copy in sent:
-            copy.wait_send()
+        settle(())
+
+    def settle(later):
+        for at, copy in enumerate(sent):
+            if at not in settled and not (later and names[at].startswith(later)):
+                copy.wait_send()
+                settled.add(at)
 
     block = pl.ds(pl.multiple_of(c * TOK, TOK), TOK)
     load_hid = pltpu.make_async_copy(hid_hbm.at[0], win.at[block, :], loc_sem.at[0])
@@ -238,7 +247,7 @@
     far = (y + NY + 2 - 4 * k) % NY
     from_block = ((c + NC - 1) % NC, (c + 1) % NC, (c + 2) % NC)
     mine = hid_hbm.at[0, pl.ds(pl.multiple_of(k * HALF, HALF), HALF), :]
-    for i, to in enumerate(((y + 1) % NY, (y + NY - 1) % NY, far)):
+    for i, to in ((2, far), (0, (y + 1) % NY), (1, (y + NY - 1) % NY)):
         send(
             f"a{i}", mine, win.at[half_rows(c, k), :], win.at[half_rows(from_block[i], k), :], at_y(to)
         )
@@ -275,22 +284,32 @@
         return carry
 
     lax.fori_loop(0, ROWS // CH, label_step, 0)
-    for n in range(NPART):
-        cols = pl.ds(n * PART, PART)
-        value = jnp.dot(g[...], w[:, n * PART : (n + 1) * PART], preferred_element_type=F32)
+
+    def part_cols(n):
+        return pl.ds(pl.multiple_of(n * PART, PART), PART)
+
+    def label_dot(n, carry):
+        cols = part_cols(n)
+        value = jnp.dot(g[...], w[:, cols], preferred_element_type=F32)
         els[:, cols] = value[: WIN // 2].astype(BF16)
         keepl[:, cols] = value[WIN // 2 :].astype(BF16)
+        return carry
+
+    lax.fori_loop(0, NPART, label_dot, 0)
     send("l", els, elr, elr, partner)
     arrived("l")
-    for j in range(NC):
-        rows = slice(j * HALF, (j + 1) * HALF)
+
+    def label_merge(j, carry):
+        rows = pl.ds(pl.multiple_of(j * HALF, HALF), HALF)
         both = (keepl[rows, :].astype(F32) + elr[rows, :].astype(F32)).astype(BF16)
         for m in range(D // 128):
             hh, zz = m // NZ, m % NZ
-            rsl[zz, hh * (NC * HALF) + j * HALF : hh * (NC * HALF) + (j + 1) * HALF, :] = both[
-                :, m * 128 : (m + 1) * 128
-            ]
-    for d in range(1, NZ):
+            rows = pl.ds(pl.multiple_of(hh * (NC * HALF) + j * HALF, HALF), HALF)
+            rsl[zz, rows, :] = both[:, m * 128 : (m + 1) * 128]
+        return carry
+
+    lax.fori_loop(0, NC, label_merge, 0)
+    for d in FAR:
         to = (z + d) % NZ
         send(f"zl{d}", rsl.at[to], rl1.at[d], rl1.at[d], at_z(to))
 
@@ -302,9 +321,16 @@
     load_hid.wait()
     for i in range(3):
         arrived(f"f{i}")
-    logit[...] = lax.dot_general(
-        w[...], win[...], (((1,), (1,)), ((), ())), preferred_element_type=F32
-    )
+    def block_rows(i):
+        return pl.ds(pl.multiple_of(i * BLOCK, BLOCK), BLOCK)
+
+    def logit_step(i, carry):
+        logit[block_rows(i), :] = lax.dot_general(
+            w[block_rows(i), :], win[...], (((1,), (1,)), ((), ())), preferred_element_type=F32
+        )
+        return carry
+
+    lax.fori_loop(0, ROWS // BLOCK, logit_step, 0)
 
     def stat_step(i, carry):
         top, label = carry
@@ -332,44 +358,62 @@
     lo, hi = pl.ds(0, SPLIT), pl.ds(SPLIT, SPLIT)
     send("q1lo", q.at[0, lo, :], q.at[1, lo, :], q.at[1, lo, :], at_x(right))
     send("q2hi", q.at[0, hi, :], q.at[2, hi, :], q.at[2, hi, :], at_x(left))
-    for n in range(NPART):
-        cols = pl.ds(n * PART, PART)
-        value = jnp.dot(g[...], w[:, n * PART : (n + 1) * PART], preferred_element_type=F32)
+    first = len(sent)
+
+    def swap(n):
+        return pltpu.make_async_remote_copy(
+            src_ref=e1s.at[:, part_cols(n)],
+            dst_ref=e1r.at[:, part_cols(n)],
+            send_sem=send_sems.at[first + n],
+            recv_sem=recv_sems.at[first + n],
+            device_id=partner,
+            device_id_type=MESH,
+        )
+
+    def weight_sums(n, carry):
+        cols = part_cols(n)
+        value = jnp.dot(g[...], w[:, cols], preferred_element_type=F32)
         e1s[:, cols] = value[: WIN // 2].astype(BF16)
         keep[:, cols] = value[WIN // 2 :]
-        send(f"e{n}", e1s.at[:, cols], e1r.at[:, cols], e1r.at[:, cols], partner)
+        swap(n).start()
+        return carry
+
+    lax.fori_loop(0, NPART, weight_sums, 0)
+    sent.extend(swap(n) for n in range(NPART))
+    names.extend("e" for n in range(NPART))
 
     arrived("c")
     pair = merge(st0, 2)
     put(sty, y, *pair)
     put(stz, z, *pair)
-    for d in range(1, NY):
+    for d in FAR:
         send(f"cy{d}", sty.at[y], sty.at[y], sty.at[(y + NY - d) % NY], at_y((y + d) % NY))
-    for d in range(1, NZ):
+    for d in FAR:
         send(f"cz{d}", stz.at[z], stz.at[z], stz.at[(z + NZ - d) % NZ], at_z((z + d) % NZ))
 
     def relative(ref, slot, norm):
         return unfold(jnp.exp(ref[slot, 0:2, :] - norm))
 
     turn([relative(st0, k, pair[0]), relative(st0, 1 - k, pair[0])], col0)
-    for n in range(NPART):
-        cols = pl.ds(n * PART, PART)
-        arrived(f"e{n}")
+
+    def pair_merge(n, carry):
+        cols = part_cols(n)
+        swap(n).wait_recv()
         for j in range(NC):
             rows = slice(j * HALF, (j + 1) * HALF)
             factors = col0[half_rows(j, k), :]
-            both = keep[rows, n * PART : (n + 1) * PART] * factors[:, 0:1]
-            both = both + e1r[rows, n * PART : (n + 1) * PART].astype(F32) * factors[:, 1:2]
+            both = keep[rows, cols] * factors[:, 0:1] + e1r[rows, cols].astype(F32) * factors[:, 1:2]
             both = both.astype(BF16)
             rsa[j, :, cols] = both[:QTR]
             for m in range(PART // 128):
-                block = n * (PART // 128) + m
-                hh, zz = block // NZ, block % NZ
-                rsb[zz, hh * TOK + j * QTR : hh * TOK + (j + 1) * QTR, :] = both[
-                    QTR:, m * 128 : (m + 1) * 128
-                ]
-
-    for d in range(1, NY):
+                hh, zz = n // (NPART // NH), n % (NPART // NH) * (PART // 128) + m
+                rows_b = pl.ds(pl.multiple_of(hh * TOK + j * QTR, QTR), QTR)
+                rsb[zz, rows_b, :] = both[QTR:, m * 128 : (m + 1) * 128]
+        return carry
+
+    lax.fori_loop(0, NPART, pair_merge, 0)
+
+    for d in FAR:
         to = (y + d) % NY
         src = rsa.at[to % NC, :, pl.ds(pl.multiple_of((to // NC) * (D // NH), D // NH), D // NH)]
         send(f"ya{d}", src, ra1.at[d], ra1.at[d], at_y(to))
@@ -377,12 +421,31 @@
         send(f"zb{d}", rsb.at[to], rb1.at[d], rb1.at[d], at_z(to))
     send("q1hi", q.at[0, hi, :], q.at[1, hi, :], q.at[1, hi, :], at_x(right))
     send("q2lo", q.at[0, lo, :], q.at[2, lo, :], q.at[2, lo, :], at_x(left))
+    for d in range(1, NY):
+        arrived(f"cy{d}")
+    ring_y = merge(sty, NY)
+    put(styz, z, *ring_y)
+    for d in FAR:
+        send(f"cyz{d}", styz.at[z], styz.at[z], styz.at[(z + NZ - d) % NZ], at_z((z + d) % NZ))
+    for d in range(1, NZ):
+        arrived(f"cz{d}")
+    ring_z = merge(stz, NZ)
+    put(stzy, y, *ring_z)
+    for d in FAR:
+        send(f"czy{d}", stzy.at[y], stzy.at[y], stzy.at[(y + NY - d) % NY], at_y((y + d) % NY))
+    turn([relative(sty, (y + NY - d) % NY, ring_y[0]) for d in range(NY)], col1a)
+    turn([relative(stz, (z + NZ - d) % NZ, ring_z[0]) for d in range(NZ)], col1b)
+
+    arrived("q1lo")
+    send("q3lo", q.at[1, lo, :], q.at[3, lo, :], q.at[3, lo, :], at_x(right))
+    arrived("q2hi")
+    send("q3hi", q.at[2, hi, :], q.at[3, hi, :], q.at[3, hi, :], at_x(left))
     own = rsl[z].astype(F32)
     for d in range(1, NZ):
         arrived(f"zl{d}")
         own = own + rl1[d].astype(F32)
     rl2s[...] = own.astype(BF16)
-    for d in range(1, NY):
+    for d in FAR:
         to = (y + d) % NY
         src = rl2s.at[pl.ds(pl.multiple_of((to // NC) * (NC * HALF) + (to % NC) * HALF, HALF), HALF), :]
         send(f"yl{d}", src, rl2.at[d], rl2.at[d], at_y(to))
@@ -394,25 +457,7 @@
             send(f"g{i}{d}", piece, piece, hc.at[place[d], half_rows(number, 1 - k), :], partner)
     hc[0] = win[:, pl.ds(pl.multiple_of(x * COLS, COLS), COLS)]
 
-    for d in range(1, NY):
-        arrived(f"cy{d}")
-    ring_y = merge(sty, NY)
-    put(styz, z, *ring_y)
-    for d in range(1, NZ):
-        send(f"cyz{d}", styz.at[z], styz.at[z], styz.at[(z + NZ - d) % NZ], at_z((z + d) % NZ))
-    for d in range(1, NZ):
-        arrived(f"cz{d}")
-    ring_z = merge(stz, NZ)
-    put(stzy, y, *ring_z)
-    for d in range(1, NY):
-        send(f"czy{d}", stzy.at[y], stzy.at[y], stzy.at[(y + NY - d) % NY], at_y((y + d) % NY))
-    turn([relative(sty, (y + NY - d) % NY, ring_y[0]) for d in range(NY)], col1a)
-    turn([relative(stz, (z + NZ - d) % NZ, ring_z[0]) for d in range(NZ)], col1b)
-
-    arrived("q1lo")
-    send("q3lo", q.at[1, lo, :], q.at[3, lo, :], q.at[3, lo, :], at_x(right))
-    arrived("q2hi")
-    send("q3hi", q.at[2, hi, :], q.at[3, hi, :], q.at[3, hi, :], at_x(left))
+    settle(("q", "ya", "zb", "cyz", "czy", "yl", "g"))
     rows_a = pl.ds(pl.multiple_of(c * TOK + k * HALF, QTR), QTR)
     rows_b = pl.ds(pl.multiple_of(c * TOK + k * HALF + QTR, QTR), QTR)
     factors = col1a[rows_a, :]
@@ -420,8 +465,8 @@
     for d in range(1, NY):
         arrived(f"ya{d}")
         own = own + ra1[d].astype(F32) * factors[:, d : d + 1]
-    ra2s[...] = own
-    for d in range(1, NZ):
+    ra2s[...] = own.astype(BF16)
+    for d in FAR:
         to = (z + d) % NZ
         src = ra2s.at[:, pl.ds(pl.multiple_of(to * 128, 128), 128)]
         send(f"za{d}", src, ra2.at[d], ra2.at[d], at_z(to))
@@ -433,11 +478,12 @@
     for d in range(1, NZ):
         arrived(f"zb{d}")
         own = own + rb1[d].astype(F32) * factors[:, d : d + 1]
-    rb2s[...] = own
-    for d in range(1, NY):
+    rb2s[...] = own.astype(BF16)
+    for d in FAR:
         to = (y + d) % NY
         src = rb2s.at[pl.ds(pl.multiple_of((to // NC) * TOK + (to % NC) * QTR, QTR), QTR), :]
         send(f"yb{d}", src, rb2.at[d], rb2.at[d], at_y(to))
+    settle(("q", "za", "yb"))
     for d in range(1, NZ):
         arrived(f"cyz{d}")
     all_top, all_rest, all_label = merge(styz, NZ)
@@ -480,6 +526,21 @@
         own = own + rl2[d].astype(F32)
     own_label = own * coll[half_rows(c, k), :][:, 0:1]
 
+    factors = col2a[rows_a, :]
+    own = own_label[:QTR]
+    own = own + ra2s[:, pl.ds(pl.multiple_of(z * 128, 128), 128)].astype(F32) * factors[:, 0:1]
+    for d in range(1, NZ):
+        arrived(f"za{d}")
+        own = own + ra2[d].astype(F32) * factors[:, d : d + 1]
+    fin[0, 0:QTR, :] = own.astype(BF16)
+    factors = col2b[rows_b, :]
+    own = own_label[QTR:]
+    own = own + rb2s[pl.ds(pl.multiple_of(h * TOK + c * QTR, QTR), QTR), :].astype(F32) * factors[:, 0:1]
+    for d in range(1, NY):
+        arrived(f"yb{d}")
+        own = own + rb2[d].astype(F32) * factors[:, d : d + 1]
+    fin[0, QTR:HALF, :] = own.astype(BF16)
+    send("fin", fin.at[0], fin.at[1], fin.at[1], partner)
     for i in range(4):
         for d in (1, 3, 2):
             arrived(f"g{i}{d}")
@@ -489,32 +550,19 @@
     near = rows_for(3)
     arrived("q2lo")
     form(2, *near)
-    acc[...] = jnp.dot(
-        gt[:, : 3 * WIN], hc[0:3].reshape(3 * WIN, COLS), preferred_element_type=F32
-    )
-
-    factors = col2a[rows_a, :]
-    own = own_label[:QTR]
-    own = own + ra2s[:, pl.ds(pl.multiple_of(z * 128, 128), 128)] * factors[:, 0:1]
-    for d in range(1, NZ):
-        arrived(f"za{d}")
-        own = own + ra2[d] * factors[:, d : d + 1]
-    fin[0, 0:QTR, :] = own.astype(BF16)
-    factors = col2b[rows_b, :]
-    own = own_label[QTR:]
-    own = own + rb2s[pl.ds(pl.multiple_of(h * TOK + c * QTR, QTR), QTR), :] * factors[:, 0:1]
-    for d in range(1, NY):
-        arrived(f"yb{d}")
-        own = own + rb2[d] * factors[:, d : d + 1]
-    fin[0, QTR:HALF, :] = own.astype(BF16)
-    send("fin", fin.at[0], fin.at[1], fin.at[1], partner)
+
     across = rows_for(2)
     arrived("q3lo")
     arrived("q3hi")
     form(3, *across)
-    head_ref[...] = (
-        acc[...] + jnp.dot(gt[:, 3 * WIN :], hc[3], preferred_element_type=F32)
-    ).astype(BF16)
+
+    def head_step(i, carry):
+        head_ref[block_rows(i), :] = jnp.dot(
+            gt[block_rows(i), :], hc[...].reshape(NX * WIN, COLS), preferred_element_type=F32
+        ).astype(BF16)
+        return carry
+
+    lax.fori_loop(0, ROWS // BLOCK, head_step, 0)
 
     arrived("fin")
     for slot, row in ((0, k), (1, 1 - k)):
@@ -557,11 +605,11 @@
             pltpu.VMEM((NY, QTR, D // NH), BF16),
             pltpu.VMEM((NZ, NH * TOK, 128), BF16),
             pltpu.VMEM((NZ, NH * NC * HALF, 128), BF16),
-            pltpu.VMEM((QTR, D // NH), F32),
-            pltpu.VMEM((NH * TOK, 128), F32),
+            pltpu.VMEM((QTR, D // NH), BF16),
+            pltpu.VMEM((NH * TOK, 128), BF16),
             pltpu.VMEM((NH * NC * HALF, 128), BF16),
-            pltpu.VMEM((NZ, QTR, 128), F32),
-            pltpu.VMEM((NY, QTR, 128), F32),
+            pltpu.VMEM((NZ, QTR, 128), BF16),
+            pltpu.VMEM((NY, QTR, 128), BF16),
             pltpu.VMEM((NY, HALF, 128), BF16),
             pltpu.VMEM((2, HALF, 128), BF16),
             pltpu.VMEM((2, 8, 128), F32),
@@ -576,7 +624,6 @@
             pltpu.VMEM((WIN, 8), F32),
             pltpu.VMEM((WIN, 8), F32),
             pltpu.VMEM((WIN, 8), F32),
-            pltpu.VMEM((ROWS, COLS), F32),
             pltpu.VMEM((1, WIN), jnp.int32),
             pltpu.VMEM((1, WIN), jnp.int32),
             pltpu.VMEM((1, WIN), jnp.int32),

time: 52.2 us -> 51.4 us (0.985)
  Pallas kernels: 50 us -> 49.1 us
    pallas_call x1, Pallas kernels: 50 us -> 49.1 us  [body(): pl.pallas_call(kernel, out_shape=(pltpu.VMEM((1, TOK, D // (NH * NZ * 2))...]
where the time goes in v4:
time: 51.4 us; the launch traced here: 51.3 us
  Pallas kernels  49.1 us (96%)
  local copies, waits for them, and re-layouts  1.53 us (3%)
  between operations  0.64 us (1%)
    pallas_call x1, Pallas kernels, body(): pl.pallas_call(kernel, out_shape=(pltpu.VMEM((1, TOK, D // (NH * NZ * 2))...  49.1 us
    unnamed x2, local copies, waits for them, and re-layouts  1.53 us

profile of v4, /device:TPU:1, one launch (start us, length us, event | category | flops | bytes accessed | tf_op | source)
XLA Modules:
  0.0 51.3 jit_solution(4425047948421797811)
XLA Ops:
  0.6 49.1 %shard_map.95 = (bf16[1,64,64]{2,1,0:T(8,128)(2,1)S(1)}, bf16[896,512]{1,0:T(8,128)(2,1)S(1)}) custom-call(bf16[1,64,2048]{2,1,0:T(8,128)(2,1)} %hid_hbm.1, bf16[896,2048]{1,0:T(8,128)(2,1)} %w_hbm.1, s32[1,256]{1,0:T(1,128)} %lab_hbm.1, s32[1,256]{1,0:T(1,128)} %mask_hbm.1, s32[1,256]{1,0:T(1,128)} %seq_hbm.1, f32[1,256]{1,0:T(1,128)} %old_hbm.1, ...), custom_call_target="tpu_custom_call" | custom-call | flops 3758096384 | bytes 4587520 | tf_op jit(solution)/shard_map/pallas_call | solution.py:580
  49.8 0.6 %copy.12 = bf16[1,64,64]{2,1,0:T(8,128)(2,1)} copy(bf16[1,64,64]{2,1,0:T(8,128)(2,1)S(1)} %get-tuple-element.2) | data formatting | bytes 16384
  50.4 0.9 %copy.13 = bf16[896,512]{1,0:T(8,128)(2,1)} copy(bf16[896,512]{1,0:T(8,128)(2,1)S(1)} %get-tuple-element.3) | data formatting | bytes 1835008

commit v5 on v4

--- a/solution.py
+++ b/solution.py
@@ -36,14 +36,18 @@
 SPLIT = ROWS // 2
 
 
-def token_weights(logp, mask, seq, old, ref, adv_ref):
-    adv = jnp.zeros_like(logp)
-    length = jnp.zeros_like(logp)
+def sequence_terms(seq, adv_ref):
+    adv = jnp.zeros(seq.shape, F32)
+    length = jnp.zeros(seq.shape, F32)
     for s in range(adv_ref.shape[1]):
         match = (seq == s).astype(F32)
         count = jnp.sum(match, axis=1, keepdims=True)
         adv = adv + match * adv_ref[0:1, s : s + 1]
         length = length + match * count
+    return adv, length
+
+
+def token_weights(logp, mask, adv, length, old, ref):
     ratio = jnp.exp(logp - old)
     low = jnp.where(ratio >= 1.0 - CLIP_LOW, jnp.where(ratio <= DUAL_CLIP, 1.0, 0.0), 0.0)
     active = jnp.where(adv >= 0.0, jnp.where(ratio <= 1.0 + CLIP_HIGH, 1.0, 0.0), low)
@@ -83,7 +87,7 @@
     return jnp.concatenate([tile[0:1, :], tile[1:2, :]], axis=1)
 
 
-SEMS = 140
+SEMS = 160
 BLOCK = 448
 FAR = (4, 3, 5, 2, 6, 1, 7)
 
@@ -115,15 +119,19 @@
     rsa,
     rsb,
     rsl,
+    rsla,
     ra1,
     rb1,
     rl1,
+    rk1,
     ra2s,
     rb2s,
     rl2s,
+    rk2s,
     ra2,
     rb2,
     rl2,
+    rk2,
     fin,
     st0,
     sty,
@@ -302,16 +310,19 @@
     def label_merge(j, carry):
         rows = pl.ds(pl.multiple_of(j * HALF, HALF), HALF)
         both = (keepl[rows, :].astype(F32) + elr[rows, :].astype(F32)).astype(BF16)
+        rsla[j] = both[:QTR]
         for m in range(D // 128):
             hh, zz = m // NZ, m % NZ
-            rows = pl.ds(pl.multiple_of(hh * (NC * HALF) + j * HALF, HALF), HALF)
-            rsl[zz, rows, :] = both[:, m * 128 : (m + 1) * 128]
+            rows = pl.ds(pl.multiple_of(hh * TOK + j * QTR, QTR), QTR)
+            rsl[zz, rows, :] = both[QTR:, m * 128 : (m + 1) * 128]
         return carry
 
     lax.fori_loop(0, NC, label_merge, 0)
     for d in FAR:
         to = (z + d) % NZ
         send(f"zl{d}", rsl.at[to], rl1.at[d], rl1.at[d], at_z(to))
+
+    adv, length = sequence_terms(seq_ref[...], adv_ref)
 
     for i in range(3):
         arrived(f"a{i}")
@@ -321,6 +332,10 @@
     load_hid.wait()
     for i in range(3):
         arrived(f"f{i}")
+    for d in FAR:
+        to = (y + d) % NY
+        src = rsla.at[to % NC, :, pl.ds(pl.multiple_of((to // NC) * (D // NH), D // NH), D // NH)]
+        send(f"yk{d}", src, rk1.at[d], rk1.at[d], at_y(to))
     def block_rows(i):
         return pl.ds(pl.multiple_of(i * BLOCK, BLOCK), BLOCK)
 
@@ -447,8 +462,17 @@
     rl2s[...] = own.astype(BF16)
     for d in FAR:
         to = (y + d) % NY
-        src = rl2s.at[pl.ds(pl.multiple_of((to // NC) * (NC * HALF) + (to % NC) * HALF, HALF), HALF), :]
+        src = rl2s.at[pl.ds(pl.multiple_of((to // NC) * TOK + (to % NC) * QTR, QTR), QTR), :]
         send(f"yl{d}", src, rl2.at[d], rl2.at[d], at_y(to))
+    own = rsla[c, :, pl.ds(pl.multiple_of(h * (D // NH), D // NH), D // NH)].astype(F32)
+    for d in range(1, NY):
+        arrived(f"yk{d}")
+        own = own + rk1[d].astype(F32)
+    rk2s[...] = own.astype(BF16)
+    for d in FAR:
+        to = (z + d) % NZ
+        src = rk2s.at[:, pl.ds(pl.multiple_of(to * 128, 128), 128)]
+        send(f"zk{d}", src, rk2.at[d], rk2.at[d], at_z(to))
 
     for i, number in ((3, c), (0, from_block[0]), (1, from_block[1]), (2, from_block[2])):
         for d in (1, 3, 2):
@@ -457,7 +481,7 @@
             send(f"g{i}{d}", piece, piece, hc.at[place[d], half_rows(number, 1 - k), :], partner)
     hc[0] = win[:, pl.ds(pl.multiple_of(x * COLS, COLS), COLS)]
 
-    settle(("q", "ya", "zb", "cyz", "czy", "yl", "g"))
+    settle(("q", "ya", "zb", "cyz", "czy", "yl", "zk", "g"))
     rows_a = pl.ds(pl.multiple_of(c * TOK + k * HALF, QTR), QTR)
     rows_b = pl.ds(pl.multiple_of(c * TOK + k * HALF + QTR, QTR), QTR)
     factors = col1a[rows_a, :]
@@ -493,7 +517,7 @@
     log_total = peak + jnp.log(whole)
     row_total = unfold(log_total)
     coeff = token_weights(
-        unfold(all_label - log_total), mask_ref[...], seq_ref[...], old_ref[...], refp_ref[...], adv_ref
+        unfold(all_label - log_total), mask_ref[...], adv, length, old_ref[...], refp_ref[...]
     )
     factor = coeff * jnp.exp(top - row_total)
     label_grad = coeff * unfold(rest / whole)
@@ -520,11 +544,15 @@
     turn([-coeff * relative(styz, (z + NZ - d) % NZ, log_total) for d in range(NZ)], col2a)
     turn([-coeff * relative(stzy, (y + NY - d) % NY, log_total) for d in range(NY)], col2b)
     turn([label_grad], coll)
-    own = rl2s[pl.ds(pl.multiple_of(h * (NC * HALF) + c * HALF, HALF), HALF), :].astype(F32)
+    own = rk2s[:, pl.ds(pl.multiple_of(z * 128, 128), 128)].astype(F32)
+    for d in range(1, NZ):
+        arrived(f"zk{d}")
+        own = own + rk2[d].astype(F32)
+    other = rl2s[pl.ds(pl.multiple_of(h * TOK + c * QTR, QTR), QTR), :].astype(F32)
     for d in range(1, NY):
         arrived(f"yl{d}")
-        own = own + rl2[d].astype(F32)
-    own_label = own * coll[half_rows(c, k), :][:, 0:1]
+        other = other + rl2[d].astype(F32)
+    own_label = jnp.concatenate([own, other], axis=0) * coll[half_rows(c, k), :][:, 0:1]
 
     factors = col2a[rows_a, :]
     own = own_label[:QTR]
@@ -601,16 +629,20 @@
             pltpu.VMEM((WIN // 2, D), BF16),
             pltpu.VMEM((NC, QTR, D), BF16),
             pltpu.VMEM((NZ, NH * TOK, 128), BF16),
-            pltpu.VMEM((NZ, NH * NC * HALF, 128), BF16),
+            pltpu.VMEM((NZ, NH * TOK, 128), BF16),
+            pltpu.VMEM((NC, QTR, D), BF16),
             pltpu.VMEM((NY, QTR, D // NH), BF16),
             pltpu.VMEM((NZ, NH * TOK, 128), BF16),
-            pltpu.VMEM((NZ, NH * NC * HALF, 128), BF16),
+            pltpu.VMEM((NZ, NH * TOK, 128), BF16),
+            pltpu.VMEM((NY, QTR, D // NH), BF16),
             pltpu.VMEM((QTR, D // NH), BF16),
             pltpu.VMEM((NH * TOK, 128), BF16),
-            pltpu.VMEM((NH * NC * HALF, 128), BF16),
+            pltpu.VMEM((NH * TOK, 128), BF16),
+            pltpu.VMEM((QTR, D // NH), BF16),
             pltpu.VMEM((NZ, QTR, 128), BF16),
             pltpu.VMEM((NY, QTR, 128), BF16),
-            pltpu.VMEM((NY, HALF, 128), BF16),
+            pltpu.VMEM((NY, QTR, 128), BF16),
+            pltpu.VMEM((NZ, QTR, 128), BF16),
             pltpu.VMEM((2, HALF, 128), BF16),
             pltpu.VMEM((2, 8, 128), F32),
             pltpu.VMEM((NY, 8, 128), F32),

time: 51.4 us -> 49.9 us (0.971)
  Pallas kernels: 49.1 us -> 47.6 us
    pallas_call x1, Pallas kernels: 49.1 us -> 47.6 us  [body(): pl.pallas_call(kernel, out_shape=(pltpu.VMEM((1, TOK, D // (NH * NZ * 2))...]
where the time goes in v5:
time: 49.9 us; the launch traced here: 49.8 us
  Pallas kernels  47.6 us (95%)
  local copies, waits for them, and re-layouts  1.53 us (3%)
  between operations  0.64 us (1%)
    pallas_call x1, Pallas kernels, body(): pl.pallas_call(kernel, out_shape=(pltpu.VMEM((1, TOK, D // (NH * NZ * 2))...  47.6 us
    unnamed x2, local copies, waits for them, and re-layouts  1.53 us

profile of v5, /device:TPU:1, one launch (start us, length us, event | category | flops | bytes accessed | tf_op | source)
XLA Modules:
  0.0 49.8 jit_solution(9746492971850711770)
XLA Ops:
  0.6 47.6 %shard_map.95 = (bf16[1,64,64]{2,1,0:T(8,128)(2,1)S(1)}, bf16[896,512]{1,0:T(8,128)(2,1)S(1)}) custom-call(bf16[1,64,2048]{2,1,0:T(8,128)(2,1)} %hid_hbm.1, bf16[896,2048]{1,0:T(8,128)(2,1)} %w_hbm.1, s32[1,256]{1,0:T(1,128)} %lab_hbm.1, s32[1,256]{1,0:T(1,128)} %mask_hbm.1, s32[1,256]{1,0:T(1,128)} %seq_hbm.1, f32[1,256]{1,0:T(1,128)} %old_hbm.1, ...), custom_call_target="tpu_custom_call" | custom-call | flops 3758096384 | bytes 4587520 | tf_op jit(solution)/shard_map/pallas_call | solution.py:608
  48.3 0.6 %copy.12 = bf16[1,64,64]{2,1,0:T(8,128)(2,1)} copy(bf16[1,64,64]{2,1,0:T(8,128)(2,1)S(1)} %get-tuple-element.2) | data formatting | bytes 16384
  48.9 0.9 %copy.13 = bf16[896,512]{1,0:T(8,128)(2,1)} copy(bf16[896,512]{1,0:T(8,128)(2,1)S(1)} %get-tuple-element.3) | data formatting | bytes 1835008

commit v6 on v5

--- a/solution.py
+++ b/solution.py
@@ -494,20 +494,6 @@
         to = (z + d) % NZ
         src = ra2s.at[:, pl.ds(pl.multiple_of(to * 128, 128), 128)]
         send(f"za{d}", src, ra2.at[d], ra2.at[d], at_z(to))
-    factors = [
-        col1b[pl.ds(pl.multiple_of(j * TOK + k * HALF + QTR, QTR), QTR), :] for j in range(NC)
-    ]
-    factors = jnp.concatenate(factors + factors, axis=0)
-    own = rsb[z].astype(F32) * factors[:, 0:1]
-    for d in range(1, NZ):
-        arrived(f"zb{d}")
-        own = own + rb1[d].astype(F32) * factors[:, d : d + 1]
-    rb2s[...] = own.astype(BF16)
-    for d in FAR:
-        to = (y + d) % NY
-        src = rb2s.at[pl.ds(pl.multiple_of((to // NC) * TOK + (to % NC) * QTR, QTR), QTR), :]
-        send(f"yb{d}", src, rb2.at[d], rb2.at[d], at_y(to))
-    settle(("q", "za", "yb"))
     for d in range(1, NZ):
         arrived(f"cyz{d}")
     all_top, all_rest, all_label = merge(styz, NZ)
@@ -525,6 +511,21 @@
     for d in (1, 3, 2):
         send(f"x{d}", scale.at[0], scale.at[d], scale.at[d], at_x((x + d) % NX))
 
+    factors = [
+        col1b[pl.ds(pl.multiple_of(j * TOK + k * HALF + QTR, QTR), QTR), :] for j in range(NC)
+    ]
+    factors = jnp.concatenate(factors + factors, axis=0)
+    own = rsb[z].astype(F32) * factors[:, 0:1]
+    for d in range(1, NZ):
+        arrived(f"zb{d}")
+        own = own + rb1[d].astype(F32) * factors[:, d : d + 1]
+    rb2s[...] = own.astype(BF16)
+    for d in FAR:
+        to = (y + d) % NY
+        src = rb2s.at[pl.ds(pl.multiple_of((to // NC) * TOK + (to % NC) * QTR, QTR), QTR), :]
+        send(f"yb{d}", src, rb2.at[d], rb2.at[d], at_y(to))
+    settle(("q", "za", "yb", "x"))
+
     def form(slot, factor_row, label_row):
         def step(i, carry):
             part = q[slot, rows_of(i), :].astype(F32)
@@ -554,6 +555,10 @@
         other = other + rl2[d].astype(F32)
     own_label = jnp.concatenate([own, other], axis=0) * coll[half_rows(c, k), :][:, 0:1]
 
+    for i in range(4):
+        for d in (1, 3, 2):
+            arrived(f"g{i}{d}")
+
     factors = col2a[rows_a, :]
     own = own_label[:QTR]
     own = own + ra2s[:, pl.ds(pl.multiple_of(z * 128, 128), 128)].astype(F32) * factors[:, 0:1]
@@ -569,9 +574,6 @@
         own = own + rb2[d].astype(F32) * factors[:, d : d + 1]
     fin[0, QTR:HALF, :] = own.astype(BF16)
     send("fin", fin.at[0], fin.at[1], fin.at[1], partner)
-    for i in range(4):
-        for d in (1, 3, 2):
-            arrived(f"g{i}{d}")
     near = rows_for(1)
     arrived("q1hi")
     form(1, *near)

time: 49.9 us -> 50.2 us (level)
  no operation moved by 1% of the time
where the time goes in v6:
time: 50.2 us; the launch traced here: 50.1 us
  Pallas kernels  47.9 us (95%)
  local copies, waits for them, and re-layouts  1.53 us (3%)
  between operations  0.64 us (1%)
    pallas_call x1, Pallas kernels, body(): pl.pallas_call(kernel, out_shape=(pltpu.VMEM((1, TOK, D // (NH * NZ * 2))...  47.9 us
    unnamed x2, local copies, waits for them, and re-layouts  1.53 us

profile of v6, /device:TPU:1, one launch (start us, length us, event | category | flops | bytes accessed | tf_op | source)
XLA Modules:
  0.0 50.1 jit_solution(6251833232507960925)
XLA Ops:
  0.6 47.9 %shard_map.95 = (bf16[1,64,64]{2,1,0:T(8,128)(2,1)S(1)}, bf16[896,512]{1,0:T(8,128)(2,1)S(1)}) custom-call(bf16[1,64,2048]{2,1,0:T(8,128)(2,1)} %hid_hbm.1, bf16[896,2048]{1,0:T(8,128)(2,1)} %w_hbm.1, s32[1,256]{1,0:T(1,128)} %lab_hbm.1, s32[1,256]{1,0:T(1,128)} %mask_hbm.1, s32[1,256]{1,0:T(1,128)} %seq_hbm.1, f32[1,256]{1,0:T(1,128)} %old_hbm.1, ...), custom_call_target="tpu_custom_call" | custom-call | flops 3758096384 | bytes 4587520 | tf_op jit(solution)/shard_map/pallas_call | solution.py:610
  48.5 0.6 %copy.12 = bf16[1,64,64]{2,1,0:T(8,128)(2,1)} copy(bf16[1,64,64]{2,1,0:T(8,128)(2,1)S(1)} %get-tuple-element.2) | data formatting | bytes 16384
  49.2 0.9 %copy.13 = bf16[896,512]{1,0:T(8,128)(2,1)} copy(bf16[896,512]{1,0:T(8,128)(2,1)S(1)} %get-tuple-element.3) | data formatting | bytes 1835008
